TPU v7x, 32 devices: a whole 2x2x4 slice. The times are simulated.
32 devices in a mesh: groups: 2 (over x), domain: 16 (over z, y, core).
Axes of the slice: x: 2, y: 2, z: 4, core: 2. Of those that a mesh axis runs over, the one named last changes fastest.
Arguments:
- state_low: float32 [8, 64, 4096], P('groups', None, 'domain'), parts along dimension 0, may hold values from -6 to 6
- state_high: float32 [8, 125, 4096], P('groups', None, 'domain'), parts along dimension 0, may hold values from -6 to 6
- forward_low: bfloat16 [4, 64, 4096], P('groups', None, 'domain'), parts along dimension 0, may hold values from -6 to 6
- forward_high: bfloat16 [4, 125, 4096], P('groups', None, 'domain'), parts along dimension 0, may hold values from -6 to 6
- bulk_modulus: float32 [8192], P('domain'), may hold values from 1 to 2
- buoyancy: float32 [8192], P('domain'), may hold values from 0.5 to 1
- stretch: float32 [8192], P('domain'), may hold values from 1 to 2
- live_count: int32 [2, 16], P(None, 'domain'), may hold values from 128 to 256, as said below
- face_link: int32 [6, 8192], P(None, 'domain'), may hold values from -1 to 4607, as said below
- send_faces: int32 [2, 12288], P(None, 'domain'), may hold values from 0 to 2943, as said below
- receiver_slot: int32 [2048], P('domain'), may hold values from 0 to 127
- residual: float32 [4, 2048], P('groups', 'domain'), parts along dimension 0, may hold values from -6 to 6
- model_cell: int32 [8192], P('domain'), may hold values from 0 to 8191, as said below
Outputs:
- adjoint_low: float32 [8, 64, 4096], P('groups', None, 'domain'), parts along dimension 0
- adjoint_high: float32 [8, 125, 4096], P('groups', None, 'domain'), parts along dimension 0
- gradient: float32 [16384], P(('groups', 'domain')), parts along dimension 0
There are 2 independent parts, one for each index of `groups`. A program takes and returns all parts, laid end to end along the dimension named above; an argument that names none is the same for every part. Nothing has to cross between parts.
Inputs may be any that keep to these rules, and one draw needn't show every extreme that they name: `live_count`: some domain index has exactly 256 live slots of each order, and some has exactly 128. `face_link`: columns from 3072 on are received ones; each of them is named by exactly one face of a slot whose number within its order is below 128 on its domain index. `send_faces`: each entry is a face column f * 2 * 256 + s of a slot whose number within its order is below 128. `model_cell`: an element of domain index d maps to a cell from (d - 2) * 512 to (d + 3) * 512 - 1.
All inputs are finite; a program needn't handle non-finite values.
Results may differ from a plain program's by a relative error of at most 0.0003.
Values sent between devices are 32-bit elements; how exact they have to be, the bound alone decides.
A program may use at most 64 MiB of HBM per device.

v0:
```python
import math

import jax
import jax.numpy as jnp
import numpy as np
from jax import lax
from jax.sharding import PartitionSpec as P

CELL_DEV = 512
STEPS = 2


HIGHEST = lax.Precision.HIGHEST
TIME_STEP = 0.02
SOURCE_WEIGHT = (45.0 / 32.0) ** 3


def padded(cells, sides, width):
    for axis, dim in sides:
        count = lax.axis_size(axis)
        ends = count - 1
        head = lax.slice_in_dim(cells, 0, width, axis=dim)
        tail = lax.slice_in_dim(cells, cells.shape[dim] - width, cells.shape[dim], axis=dim)
        cells = jnp.concatenate(
            [
                lax.ppermute(tail, axis, [(i, (i + 1) % count) for i in range(ends)]),
                cells,
                lax.ppermute(head, axis, [((i + 1) % count, i) for i in range(ends)]),
            ],
            axis=dim,
        )
    return cells


def shifted(block, axis, distance):
    devices = range(lax.axis_size(axis))
    route = [(i - distance, i) for i in devices if i - distance in devices]
    return lax.ppermute(block, axis, route)


def gll_points(degree):
    if degree == 3:
        interior = math.sqrt(0.2)
        return np.array([-1.0, -interior, interior, 1.0])
    interior = math.sqrt(3.0 / 7.0)
    return np.array([-1.0, -interior, 0.0, interior, 1.0])


def gll_weights(degree):
    if degree == 3:
        return np.array([1.0 / 6.0, 5.0 / 6.0, 5.0 / 6.0, 1.0 / 6.0])
    return np.array([0.1, 49.0 / 90.0, 32.0 / 45.0, 49.0 / 90.0, 0.1])


def lagrange_table(targets, sources):
    result = np.ones((targets.shape[0], sources.shape[0]))
    for col_index in range(sources.shape[0]):
        for skip_index in range(sources.shape[0]):
            if skip_index != col_index:
                result[:, col_index] *= (targets - sources[skip_index]) / (
                    sources[col_index] - sources[skip_index]
                )
    return result


def derivative_table(degree):
    points = gll_points(degree)
    number = points.shape[0]
    barycentric = np.ones(number)
    for col_index in range(number):
        for skip_index in range(number):
            if skip_index != col_index:
                barycentric[col_index] /= points[col_index] - points[skip_index]
    result = np.zeros((number, number))
    for row_index in range(number):
        for col_index in range(number):
            if row_index != col_index:
                result[row_index, col_index] = (
                    barycentric[col_index]
                    / barycentric[row_index]
                    / (points[row_index] - points[col_index])
                )
        result[row_index, row_index] = -np.sum(result[row_index])
    return result


def cube_weights(weights):
    return (weights[:, None, None] * weights[None, :, None] * weights[None, None, :]).reshape(-1)


def basis_tables():
    low_points = gll_points(3)
    high_points = gll_points(4)
    weight_low = cube_weights(gll_weights(3))
    weight_high = cube_weights(gll_weights(4))
    return (
        jnp.asarray(derivative_table(3), jnp.float32),
        jnp.asarray(derivative_table(4), jnp.float32),
        jnp.asarray(lagrange_table(high_points, low_points), jnp.float32),
        jnp.asarray(lagrange_table(low_points, high_points), jnp.float32),
        jnp.asarray(weight_low, jnp.float32),
        jnp.asarray(weight_high, jnp.float32),
    )


def derive_along(matrix, field, direction):
    patterns = ("ai,ijke->ajke", "aj,ijke->iake", "ak,ijke->ijae")
    return jnp.einsum(patterns[direction], matrix, field, precision=HIGHEST)


def face_stack(field):
    return jnp.stack(
        [field[0], field[-1], field[:, 0], field[:, -1], field[:, :, 0], field[:, :, -1]], axis=2
    )


def normal_stack(velocity):
    return jnp.stack(
        [
            -velocity[0][0],
            velocity[0][-1],
            -velocity[1][:, 0],
            velocity[1][:, -1],
            -velocity[2][:, :, 0],
            velocity[2][:, :, -1],
        ],
        axis=2,
    )


def to_mortar(faces_low, faces_high):
    raise_map = basis_tables()[2]
    lifted = jnp.einsum("ai,bj,ijfe->abfe", raise_map, raise_map, faces_low, precision=HIGHEST)
    joined = jnp.concatenate([lifted, faces_high], axis=3)
    return joined.reshape(25, -1)


def from_mortar(jump, slot_total):
    lower_map = basis_tables()[3]
    shaped = jump.reshape(5, 5, 6, 2 * slot_total)
    jump_low = jnp.einsum(
        "ia,jb,abfe->ijfe", lower_map, lower_map, shaped[..., :slot_total], precision=HIGHEST
    )
    return (jump_low, shaped[..., slot_total:])


def neighbour_traces(own_traces, remote, face_link):
    trace_table = jnp.concatenate([own_traces, remote], axis=1)
    flat_link = face_link.reshape(-1)
    picked = jnp.take(trace_table, jnp.maximum(flat_link, 0), axis=1)
    return jnp.where(flat_link >= 0, picked, 0.0)


def place_faces(direction, low_face, high_face):
    extent = low_face.shape[0]
    empty_field = jnp.zeros((extent, extent, extent, low_face.shape[-1]), jnp.float32)
    if direction == 0:
        return empty_field.at[0].add(low_face).at[extent - 1].add(high_face)
    if direction == 1:
        return empty_field.at[:, 0].add(low_face).at[:, extent - 1].add(high_face)
    return empty_field.at[:, :, 0].add(low_face).at[:, :, extent - 1].add(high_face)


def move_velocity(pressure, velocity, jump, matrix, lift_scale, buoyancy, stretch, alive_mask):
    updated = []
    for direction in range(3):
        gradient_part = derive_along(matrix, pressure, direction) + lift_scale * place_faces(
            direction, -jump[:, :, 2 * direction], jump[:, :, 2 * direction + 1]
        )
        updated.append(velocity[direction] - TIME_STEP * buoyancy * stretch * gradient_part)
    return jnp.stack(updated) * alive_mask


def move_pressure(pressure, velocity, jump, matrix, lift_scale, bulk_modulus, stretch, alive_mask):
    spread = (
        derive_along(matrix, velocity[0], 0)
        + derive_along(matrix, velocity[1], 1)
        + derive_along(matrix, velocity[2], 2)
    )
    for direction in range(3):
        spread = spread + lift_scale * place_faces(
            direction, jump[:, :, 2 * direction], jump[:, :, 2 * direction + 1]
        )
    return (pressure - TIME_STEP * bulk_modulus * stretch * spread) * alive_mask


def start_state(state_low, state_high, live_count):
    slot_total = state_low.shape[2]
    alive_low = (jnp.arange(slot_total) < live_count[0, 0]).astype(jnp.float32)
    alive_high = (jnp.arange(slot_total) < live_count[1, 0]).astype(jnp.float32)
    pressure_low = state_low[0].reshape(4, 4, 4, slot_total) * alive_low
    velocity_low = state_low[1:].reshape(3, 4, 4, 4, slot_total) * alive_low
    pressure_high = state_high[0].reshape(5, 5, 5, slot_total) * alive_high
    velocity_high = state_high[1:].reshape(3, 5, 5, 5, slot_total) * alive_high
    return (pressure_low, velocity_low, pressure_high, velocity_high, alive_low, alive_high)


def pressure_traces(pressure_low, pressure_high):
    return to_mortar(face_stack(pressure_low), face_stack(pressure_high))


def velocity_traces(velocity_low, velocity_high):
    return to_mortar(normal_stack(velocity_low), normal_stack(velocity_high))


def pick_sent(own_traces, send_faces):
    return jnp.take(own_traces, send_faces.reshape(-1), axis=1).reshape(own_traces.shape[0], 2, -1)


def velocity_half(
    pressure_low,
    velocity_low,
    pressure_high,
    velocity_high,
    own_traces,
    remote,
    face_link,
    buoyancy,
    stretch,
    alive_low,
    alive_high,
):
    derivative_low, derivative_high = basis_tables()[:2]
    slot_total = pressure_low.shape[-1]
    jump = 0.5 * (neighbour_traces(own_traces, remote, face_link) - own_traces)
    jump_low, jump_high = from_mortar(jump, slot_total)
    velocity_low = move_velocity(
        pressure_low,
        velocity_low,
        jump_low,
        derivative_low,
        6.0,
        buoyancy[:slot_total],
        stretch[:slot_total],
        alive_low,
    )
    velocity_high = move_velocity(
        pressure_high,
        velocity_high,
        jump_high,
        derivative_high,
        10.0,
        buoyancy[slot_total:],
        stretch[slot_total:],
        alive_high,
    )
    return (velocity_low, velocity_high)


def pressure_half(
    pressure_low,
    velocity_low,
    pressure_high,
    velocity_high,
    own_traces,
    remote,
    face_link,
    bulk_modulus,
    stretch,
    alive_low,
    alive_high,
    receiver_slot,
    residual_now,
    forward_low_now,
    forward_high_now,
):
    derivative_low, derivative_high, raise_map, lower_map, weight_low, weight_high = basis_tables()
    slot_total = pressure_low.shape[-1]
    jump = -0.5 * (neighbour_traces(own_traces, remote, face_link) + own_traces)
    jump_low, jump_high = from_mortar(jump, slot_total)
    stretch_low = stretch[:slot_total]
    stretch_high = stretch[slot_total:]
    modulus_high = bulk_modulus[slot_total:]
    pressure_low = move_pressure(
        pressure_low,
        velocity_low,
        jump_low,
        derivative_low,
        6.0,
        bulk_modulus[:slot_total],
        stretch_low,
        alive_low,
    )
    pressure_high = move_pressure(
        pressure_high,
        velocity_high,
        jump_high,
        derivative_high,
        10.0,
        modulus_high,
        stretch_high,
        alive_high,
    )
    source = jnp.zeros((slot_total,), jnp.float32).at[receiver_slot].add(residual_now)
    pressure_high = pressure_high.at[2, 2, 2].add(
        TIME_STEP * SOURCE_WEIGHT * modulus_high * stretch_high**3 * source
    )
    term_low = (
        jnp.dot(
            weight_low,
            forward_low_now.astype(jnp.float32) * pressure_low.reshape(-1, slot_total),
            precision=HIGHEST,
        )
        / stretch_low**3
    )
    term_high = (
        jnp.dot(
            weight_high,
            forward_high_now.astype(jnp.float32) * pressure_high.reshape(-1, slot_total),
            precision=HIGHEST,
        )
        / stretch_high**3
    )
    return (pressure_low, pressure_high, jnp.concatenate([term_low, term_high]))


def final_state(pressure, velocity):
    slot_total = pressure.shape[-1]
    return jnp.concatenate(
        [pressure.reshape(1, -1, slot_total), velocity.reshape(3, -1, slot_total)], axis=0
    )


def trade_pressure(outgoing):
    widened = padded(outgoing, (("domain", 1),), 1)
    return jnp.concatenate([widened[:, 0], widened[:, 3]], axis=1)


def trade_velocity(outgoing):
    widened = padded(outgoing, (("domain", 1),), 1)
    return jnp.concatenate([widened[:, 0], widened[:, 3]], axis=1)


def shards(
    state_low,
    state_high,
    forward_low,
    forward_high,
    bulk_modulus,
    buoyancy,
    stretch,
    live_count,
    face_link,
    send_faces,
    receiver_slot,
    residual,
    model_cell,
):
    started = start_state(state_low, state_high, live_count)
    pressure_low, velocity_low, pressure_high, velocity_high, alive_low, alive_high = started
    element_terms = jnp.zeros(bulk_modulus.shape, jnp.float32)
    for time_step in range(STEPS):
        own_traces = pressure_traces(pressure_low, pressure_high)
        remote = trade_pressure(pick_sent(own_traces, send_faces))
        velocity_low, velocity_high = velocity_half(
            pressure_low,
            velocity_low,
            pressure_high,
            velocity_high,
            own_traces,
            remote,
            face_link,
            buoyancy,
            stretch,
            alive_low,
            alive_high,
        )
        own_traces = velocity_traces(velocity_low, velocity_high)
        remote = trade_velocity(pick_sent(own_traces, send_faces))
        pressure_low, pressure_high, new_terms = pressure_half(
            pressure_low,
            velocity_low,
            pressure_high,
            velocity_high,
            own_traces,
            remote,
            face_link,
            bulk_modulus,
            stretch,
            alive_low,
            alive_high,
            receiver_slot,
            residual[time_step],
            forward_low[time_step],
            forward_high[time_step],
        )
        element_terms = element_terms + new_terms
    adjoint_low = final_state(pressure_low, velocity_low)
    adjoint_high = final_state(pressure_high, velocity_high)
    window_base = (lax.axis_index("domain") - 2) * CELL_DEV
    window = jnp.zeros((5 * CELL_DEV,), jnp.float32).at[model_cell - window_base].add(element_terms)
    gradient = window[2 * CELL_DEV : 3 * CELL_DEV]
    for distance in (-2, -1, 1, 2):
        block = window[(distance + 2) * CELL_DEV : (distance + 3) * CELL_DEV]
        gradient = gradient + shifted(block, "domain", distance)
    return (adjoint_low, adjoint_high, gradient)


def solution(mesh):
    placed = (
        P("groups", None, "domain"),
        P("groups", None, "domain"),
        P("groups", None, "domain"),
        P("groups", None, "domain"),
        P("domain"),
        P("domain"),
        P("domain"),
        P(None, "domain"),
        P(None, "domain"),
        P(None, "domain"),
        P("domain"),
        P("groups", "domain"),
        P("domain"),
    )
    return jax.shard_map(
        shards,
        mesh=mesh,
        in_specs=placed,
        out_specs=(
            P("groups", None, "domain"),
            P("groups", None, "domain"),
            P(("groups", "domain")),
        ),
        check_vma=False,
    )
```

profile of v0, /device:TPU:19, one launch (start us, length us, event | category | flops | bytes accessed | tf_op | source)
XLA Modules:
  0.0 183.8 jit_solution(5598933601107120297)
XLA Ops:
  1.4 1.3 fusion.204
  5.1 1.4 slice_reduce_fusion
  8.8 2.6 %gather_fusion = f32[1536,25]{1,0:T(8,128)S(1)} fusion(f32[25,3072]{0,1:T(8,128)S(1)} %copy.796, s32[2048]{0:T(1024)S(1)} %pad_clamp_fusion), kind=kCustom, calls=%fused_computation.clone | custom fusion | bytes 313344 | tf_op jit(solution)/shard_map/jit(_take)/gather | solution.py:207
  12.0 2.7 %collective-permute-start.1 = (f32[25,1,768]{2,0,1:T(8,128)S(1)}, f32[25,1,768]{2,0,1:T(8,128)S(1)}, u32[]{:S(2)}, u32[]{:S(2)}) collective-permute-start(f32[25,1,768]{2,0,1:T(8,128)S(1)} %copy.951), channel_id=1, source_target_pairs={{1,0},{2,1},{3,2},{4,3},{5,4},{6,5},{7,6},{8,7},{9,8},{10,9},{11,1... | collective-permute-start | bytes 230408 | tf_op jit(solution)/shard_map/ppermute | solution.py:28
  14.9 3.0 %collective-permute-start = (f32[25,1,768]{2,0,1:T(8,128)S(1)}, f32[25,1,768]{2,0,1:T(8,128)S(1)}, u32[]{:S(2)}, u32[]{:S(2)}) collective-permute-start(f32[25,1,768]{2,0,1:T(8,128)S(1)} %copy.950), channel_id=1, source_target_pairs={{0,1},{1,2},{2,3},{3,4},{4,5},{5,6},{6,7},{7,8},{8,9},{9,10},{10,1... | collective-permute-start | bytes 230408 | tf_op jit(solution)/shard_map/ppermute | solution.py:26
  19.0 1.4 scatter_custom_fusion.1
  20.4 1.4 scatter_custom_fusion
  24.4 0.9 copy_multiply_fusion
  27.4 1.8 copy.799
  29.2 10.8 %gather_fusion.1 = f32[3072,25]{1,0:T(8,128)} fusion(f32[25,4608]{0,1:T(8,128)S(1)} %copy.799, s32[3072]{0:T(1024)S(1)} %fusion.155), kind=kCustom, calls=%fused_computation.1.clone | custom fusion | bytes 626688 | tf_op jit(solution)/shard_map/jit(_take)/gather | solution.py:150
  40.0 1.9 %copy.800 = f32[3072,25]{0,1:T(8,128)S(1)} copy(f32[3072,25]{1,0:T(8,128)} %gather_fusion.1) | data formatting | bytes 614400 | tf_op jit(solution)/shard_map/jit(_take)/gather | solution.py:150
  48.7 1.0 fusion.76
  50.8 3.7 %gather_fusion.2 = f32[1536,25]{1,0:T(8,128)} fusion(f32[25,3072]{0,1:T(8,128)S(1)} %copy.844, s32[2048]{0:T(1024)S(1)} %pad_clamp_fusion), kind=kCustom, calls=%fused_computation.2.clone | custom fusion | bytes 313344 | tf_op jit(solution)/shard_map/jit(_take)/gather | solution.py:207
  54.5 1.4 broadcast_select_fusion.2
  56.3 1.9 %collective-permute-start.3 = (f32[25,1,768]{2,0,1:T(8,128)S(1)}, f32[25,1,768]{2,0,1:T(8,128)S(1)}, u32[]{:S(2)}, u32[]{:S(2)}) collective-permute-start(f32[25,1,768]{2,0,1:T(8,128)S(1)} %copy.964), channel_id=1, source_target_pairs={{1,0},{2,1},{3,2},{4,3},{5,4},{6,5},{7,6},{8,7},{9,8},{10,9},{11,1... | collective-permute-start | bytes 230408 | tf_op jit(solution)/shard_map/ppermute | solution.py:28
  58.2 3.6 %collective-permute-start.2 = (f32[25,1,768]{2,0,1:T(8,128)S(1)}, f32[25,1,768]{2,0,1:T(8,128)S(1)}, u32[]{:S(2)}, u32[]{:S(2)}) collective-permute-start(f32[25,1,768]{2,0,1:T(8,128)S(1)} %copy.963), channel_id=1, source_target_pairs={{0,1},{1,2},{2,3},{3,4},{4,5},{5,6},{6,7},{7,8},{8,9},{9,10},{10,1... | collective-permute-start | bytes 230408 | tf_op jit(solution)/shard_map/ppermute | solution.py:26
  62.7 1.6 collective-permute-done.2
  65.2 1.8 copy.847
  67.0 10.8 %gather_fusion.3 = f32[3072,25]{1,0:T(8,128)} fusion(f32[25,4608]{0,1:T(8,128)S(1)} %copy.847, s32[3072]{0:T(1024)S(1)} %fusion.155), kind=kCustom, calls=%fused_computation.5.clone | custom fusion | bytes 626688 | tf_op jit(solution)/shard_map/jit(_take)/gather | solution.py:150
  77.8 1.9 %copy.848 = f32[3072,25]{0,1:T(8,128)S(1)} copy(f32[3072,25]{1,0:T(8,128)} %gather_fusion.3) | data formatting | bytes 614400 | tf_op jit(solution)/shard_map/jit(_take)/gather | solution.py:150
  82.7 0.9 fusion.175
  84.7 1.0 fusion.181
  85.7 1.0 fusion.74
  88.9 3.7 %gather_fusion.4 = f32[1536,25]{1,0:T(8,128)} fusion(f32[25,3072]{0,1:T(8,128)S(1)} %copy.879, s32[2048]{0:T(1024)S(1)} %pad_clamp_fusion), kind=kCustom, calls=%fused_computation.3.clone | custom fusion | bytes 313344 | tf_op jit(solution)/shard_map/jit(_take)/gather | solution.py:207
  92.6 1.4 broadcast_select_fusion.1
  94.4 5.0 %collective-permute-start.5 = (f32[25,1,768]{2,0,1:T(8,128)S(1)}, f32[25,1,768]{2,0,1:T(8,128)S(1)}, u32[]{:S(2)}, u32[]{:S(2)}) collective-permute-start(f32[25,1,768]{2,0,1:T(8,128)S(1)} %copy.975), channel_id=1, source_target_pairs={{1,0},{2,1},{3,2},{4,3},{5,4},{6,5},{7,6},{8,7},{9,8},{10,9},{11,1... | collective-permute-start | bytes 230408 | tf_op jit(solution)/shard_map/ppermute | solution.py:28
  99.4 2.1 %collective-permute-start.4 = (f32[25,1,768]{2,0,1:T(8,128)S(1)}, f32[25,1,768]{2,0,1:T(8,128)S(1)}, u32[]{:S(2)}, u32[]{:S(2)}) collective-permute-start(f32[25,1,768]{2,0,1:T(8,128)S(1)} %copy.974), channel_id=1, source_target_pairs={{0,1},{1,2},{2,3},{3,4},{4,5},{5,6},{6,7},{7,8},{8,9},{9,10},{10,1... | collective-permute-start | bytes 230408 | tf_op jit(solution)/shard_map/ppermute | solution.py:26
  104.0 1.8 copy.882
  105.8 10.8 %gather_fusion.5 = f32[3072,25]{1,0:T(8,128)} fusion(f32[25,4608]{0,1:T(8,128)S(1)} %copy.882, s32[3072]{0:T(1024)S(1)} %fusion.155), kind=kCustom, calls=%fused_computation.6.clone | custom fusion | bytes 626688 | tf_op jit(solution)/shard_map/jit(_take)/gather | solution.py:150
  116.7 1.9 %copy.883 = f32[3072,25]{0,1:T(8,128)S(1)} copy(f32[3072,25]{1,0:T(8,128)} %gather_fusion.5) | data formatting | bytes 614400 | tf_op jit(solution)/shard_map/jit(_take)/gather | solution.py:150
  127.7 1.0 fusion.70
  128.8 1.0 fusion.68
  130.9 2.6 %gather_fusion.6 = f32[1536,25]{1,0:T(8,128)S(1)} fusion(f32[25,3072]{0,1:T(8,128)S(1)} %copy.914, s32[2048]{0:T(1024)S(1)} %pad_clamp_fusion), kind=kCustom, calls=%fused_computation.4.clone | custom fusion | bytes 313344 | tf_op jit(solution)/shard_map/jit(_take)/gather | solution.py:207
  134.3 5.0 %collective-permute-start.7 = (f32[25,1,768]{2,0,1:T(8,128)S(1)}, f32[25,1,768]{2,0,1:T(8,128)S(1)}, u32[]{:S(2)}, u32[]{:S(2)}) collective-permute-start(f32[25,1,768]{2,0,1:T(8,128)S(1)} %copy.987), channel_id=1, source_target_pairs={{1,0},{2,1},{3,2},{4,3},{5,4},{6,5},{7,6},{8,7},{9,8},{10,9},{11,1... | collective-permute-start | bytes 230408 | tf_op jit(solution)/shard_map/ppermute | solution.py:28
  139.3 1.9 %collective-permute-start.6 = (f32[25,1,768]{2,0,1:T(8,128)S(1)}, f32[25,1,768]{2,0,1:T(8,128)S(1)}, u32[]{:S(2)}, u32[]{:S(2)}) collective-permute-start(f32[25,1,768]{2,0,1:T(8,128)S(1)} %copy.986), channel_id=1, source_target_pairs={{0,1},{1,2},{2,3},{3,4},{4,5},{5,6},{6,7},{7,8},{8,9},{9,10},{10,1... | collective-permute-start | bytes 230408 | tf_op jit(solution)/shard_map/ppermute | solution.py:26
  142.0 0.9 fusion.118
  143.9 1.8 copy.917
  145.7 10.8 %gather_fusion.7 = f32[3072,25]{1,0:T(8,128)} fusion(f32[25,4608]{0,1:T(8,128)S(1)} %copy.917, s32[3072]{0:T(1024)S(1)} %fusion.155), kind=kCustom, calls=%fused_computation.7.clone | custom fusion | bytes 626688 | tf_op jit(solution)/shard_map/jit(_take)/gather | solution.py:150
  156.5 1.9 %copy.918 = f32[3072,25]{0,1:T(8,128)S(1)} copy(f32[3072,25]{1,0:T(8,128)} %gather_fusion.7) | data formatting | bytes 614400 | tf_op jit(solution)/shard_map/jit(_take)/gather | solution.py:150
  159.7 1.1 fusion.43
  161.4 1.4 fusion.22
  163.4 3.4 %scatter_custom_fusion.2 = f32[2560]{0:T(1024)S(1)} fusion(s32[512]{0:T(512)} %compare_select_fusion.2, f32[512]{0:T(512)S(1)} %maximum_add_fusion, f32[]{:T(128)} %constant.1110.clone.1), kind=kCustom, calls=%fused_computation.367 | custom fusion | flops 512 | bytes 10752 | tf_op jit(solution)/shard_map/scatter-add | solution.py:391
  166.8 4.0 %collective-permute-start.8 = (f32[512]{0:T(512)S(1)}, f32[512]{0:T(512)S(1)}, u32[]{:S(2)}, u32[]{:S(2)}) collective-permute-start(f32[512]{0:T(512)S(1)} %get-tuple-element.715), channel_id=1, source_target_pairs={{2,0},{3,1},{4,2},{5,3},{6,4},{7,5},{8,6},{9,7},{10,8},{11,9},{12,... | collective-permute-start | bytes 6152 | tf_op jit(solution)/shard_map/ppermute | solution.py:38
  170.8 2.0 %collective-permute-start.11 = (f32[512]{0:T(512)S(1)}, f32[512]{0:T(512)S(1)}, u32[]{:S(2)}, u32[]{:S(2)}) collective-permute-start(f32[512]{0:T(512)S(1)} %get-tuple-element.716), channel_id=1, source_target_pairs={{0,2},{1,3},{2,4},{3,5},{4,6},{5,7},{6,8},{7,9},{8,10},{9,11},{10,... | collective-permute-start | bytes 6152 | tf_op jit(solution)/shard_map/ppermute | solution.py:38
  172.8 5.4 %collective-permute-start.10 = (f32[512]{0:T(512)S(1)}, f32[512]{0:T(512)S(1)}, u32[]{:S(2)}, u32[]{:S(2)}) collective-permute-start(f32[512]{0:T(512)S(1)} %get-tuple-element.717), channel_id=1, source_target_pairs={{0,1},{1,2},{2,3},{3,4},{4,5},{5,6},{6,7},{7,8},{8,9},{9,10},{10,1... | collective-permute-start | bytes 6152 | tf_op jit(solution)/shard_map/ppermute | solution.py:38
  178.3 1.9 %collective-permute-start.9 = (f32[512]{0:T(512)S(1)}, f32[512]{0:T(512)S(1)}, u32[]{:S(2)}, u32[]{:S(2)}) collective-permute-start(f32[512]{0:T(512)S(1)} %get-tuple-element.718), channel_id=1, source_target_pairs={{1,0},{2,1},{3,2},{4,3},{5,4},{6,5},{7,6},{8,7},{9,8},{10,9},{11,1... | collective-permute-start | bytes 6152 | tf_op jit(solution)/shard_map/ppermute | solution.py:38
  181.0 1.1 copy.942
  182.1 1.1 collective-permute-done.9
  (487 shorter events, 44.9 us)
Async XLA Ops:
  0.6 6.2 %copy-start.42 = (f32[5,4,1,1]{0,1,3,2:T(4,128)S(1)}, f32[5,4,1,1]{0,1,3,2:T(4,128)}, u32[]{:S(2)}) copy-start(f32[5,4,1,1]{0,1,3,2:T(4,128)} %constant.1180) | copy-start | bytes 244
  1.4 10.1 %copy-start.54 = (pred[1536]{0:T(1024)(128)(4,1)}, pred[1536]{0:T(1024)(128)(4,1)S(1)}, u32[]{:S(2)}) copy-start(pred[1536]{0:T(1024)(128)(4,1)S(1)} %compare_and_fusion.1) | copy-start | bytes 4612
  3.4 19.4 %copy-start.58 = (f32[256]{0:T(256)}, f32[256]{0:T(256)S(1)}, u32[]{:S(2)}) copy-start(f32[256]{0:T(256)S(1)} %compare_convert_fusion.1) | copy-start | bytes 3076
  5.0 19.3 %copy-start.63 = (f32[256]{0:T(256)}, f32[256]{0:T(256)S(1)}, u32[]{:S(2)}) copy-start(f32[256]{0:T(256)S(1)} %compare_convert_fusion) | copy-start | bytes 3076
  11.7 6.2 %copy-start.53 = (s32[6,512]{1,0:T(8,128)S(1)}, s32[6,512]{1,0:T(8,128)}, u32[]{:S(2)}) copy-start(s32[6,512]{1,0:T(8,128)} %param.145) | copy-start | bytes 36868
  11.7 6.3 %copy-start.27 = (f32[5,5,1,1]{1,0,3,2:T(8,128)S(1)}, f32[5,5,1,1]{1,0,3,2:T(8,128)}, u32[]{:S(2)}) copy-start(f32[5,5,1,1]{1,0,3,2:T(8,128)} %constant.1182) | copy-start | bytes 304
  11.7 7.0 %copy-start.12 = (f32[4,125,256]{2,0,1:T(4,128)S(1)}, f32[4,125,256]{2,0,1:T(4,128)}, u32[]{:S(2)}) copy-start(f32[4,125,256]{2,0,1:T(4,128)} %param.138) | copy-start | bytes 1536004
  11.8 7.1 %copy-start.90 = (s32[128]{0:T(128)S(1)}, s32[128]{0:T(128)}, u32[]{:S(2)}) copy-start(s32[128]{0:T(128)} %param.147) | copy-start | bytes 1540
  11.8 7.1 %copy-start.89 = (f32[2,128]{1,0:T(2,128)S(1)}, f32[2,128]{1,0:T(2,128)}, u32[]{:S(2)}) copy-start(f32[2,128]{1,0:T(2,128)} %param.148) | copy-start | bytes 3076
  11.8 10.0 %copy-start.24 = (f32[4,4,1,1]{1,0,3,2:T(4,128)S(1)}, f32[4,4,1,1]{1,0,3,2:T(4,128)}, u32[]{:S(2)}) copy-start(f32[4,4,1,1]{1,0,3,2:T(4,128)} %constant.1179) | copy-start | bytes 196
  12.0 10.7 %slice-start = ((f32[4,64,256]{2,1,0:T(8,128)}), f32[3,64,256]{2,1,0:T(8,128)S(1)}, s32[]{:S(2)}) async-start(f32[4,64,256]{2,1,0:T(8,128)} %param.137), calls=%async_computation | async-start | bytes 393216 | tf_op jit(solution)/shard_map/slice | solution.py:192
  12.0 14.5 %collective-permute-start.1 = (f32[25,1,768]{2,0,1:T(8,128)S(1)}, f32[25,1,768]{2,0,1:T(8,128)S(1)}, u32[]{:S(2)}, u32[]{:S(2)}) collective-permute-start(f32[25,1,768]{2,0,1:T(8,128)S(1)} %copy.951), channel_id=1, source_target_pairs={{1,0},{2,1},{3,2},{4,3},{5,4},{6,5},{7,6},{8,7},{9,8},{10,9},{11,1... | collective-permute-start | bytes 230408 | tf_op jit(solution)/shard_map/ppermute | solution.py:28
  14.9 11.7 %collective-permute-start = (f32[25,1,768]{2,0,1:T(8,128)S(1)}, f32[25,1,768]{2,0,1:T(8,128)S(1)}, u32[]{:S(2)}, u32[]{:S(2)}) collective-permute-start(f32[25,1,768]{2,0,1:T(8,128)S(1)} %copy.950), channel_id=1, source_target_pairs={{0,1},{1,2},{2,3},{3,4},{4,5},{5,6},{6,7},{7,8},{8,9},{9,10},{10,1... | collective-permute-start | bytes 230408 | tf_op jit(solution)/shard_map/ppermute | solution.py:26
  18.0 23.9 %copy-start.43 = (pred[3072]{0:T(1024)(128)(4,1)}, pred[3072]{0:T(1024)(128)(4,1)S(1)}, u32[]{:S(2)}) copy-start(pred[3072]{0:T(1024)(128)(4,1)S(1)} %compare_and_fusion) | copy-start | bytes 9220
  18.0 5.5 %copy-start.23 = (bf16[2,125,256]{2,0,1:T(2,128)(2,1)S(1)}, bf16[2,125,256]{2,0,1:T(2,128)(2,1)}, u32[]{:S(2)}) copy-start(bf16[2,125,256]{2,0,1:T(2,128)(2,1)} %param.140) | copy-start | bytes 384004
  18.9 6.5 %copy-start.76 = (f32[512]{0:T(512)S(1)}, f32[512]{0:T(512)}, u32[]{:S(2)}) copy-start(f32[512]{0:T(512)} %param.143) | copy-start | bytes 6148
  18.9 6.4 %copy-start.86 = (f32[512]{0:T(512)S(1)}, f32[512]{0:T(512)}, u32[]{:S(2)}) copy-start(f32[512]{0:T(512)} %param.141) | copy-start | bytes 6148
  18.9 6.4 %copy-start.87 = (f32[512]{0:T(512)S(1)}, f32[512]{0:T(512)}, u32[]{:S(2)}) copy-start(f32[512]{0:T(512)} %param.142) | copy-start | bytes 6148
  18.9 7.0 %copy-start.88 = (s32[512]{0:T(512)S(1)}, s32[512]{0:T(512)}, u32[]{:S(2)}) copy-start(s32[512]{0:T(512)} %param.149) | copy-start | bytes 6148
  22.8 3.8 %copy-start.14 = (f32[3,4,4,4,256]{4,3,2,1,0:T(4,128)}, f32[3,4,4,4,256]{4,3,2,1,0:T(4,128)S(1)}, u32[]{:S(2)}) copy-start(f32[3,4,4,4,256]{4,3,2,1,0:T(4,128)S(1)} %broadcast_multiply_fusion) | copy-start | bytes 589828
  50.3 14.1 %copy-start.2 = (f32[4,8,6,512]{3,1,2,0:T(8,128)}, f32[4,8,6,512]{3,1,2,0:T(8,128)S(1)}, u32[]{:S(2)}) copy-start(f32[4,8,6,512]{3,1,2,0:T(8,128)S(1)} %copy.1004) | copy-start | bytes 1179652
  50.3 4.2 %copy-start.55 = (pred[1536]{0:T(1024)(128)(4,1)S(1)}, pred[1536]{0:T(1024)(128)(4,1)}, u32[]{:S(2)}) copy-start(pred[1536]{0:T(1024)(128)(4,1)} %copy-done.54) | copy-start | bytes 4612
  56.3 6.4 %collective-permute-start.3 = (f32[25,1,768]{2,0,1:T(8,128)S(1)}, f32[25,1,768]{2,0,1:T(8,128)S(1)}, u32[]{:S(2)}, u32[]{:S(2)}) collective-permute-start(f32[25,1,768]{2,0,1:T(8,128)S(1)} %copy.964), channel_id=1, source_target_pairs={{1,0},{2,1},{3,2},{4,3},{5,4},{6,5},{7,6},{8,7},{9,8},{10,9},{11,1... | collective-permute-start | bytes 230408 | tf_op jit(solution)/shard_map/ppermute | solution.py:28
  58.2 6.1 %collective-permute-start.2 = (f32[25,1,768]{2,0,1:T(8,128)S(1)}, f32[25,1,768]{2,0,1:T(8,128)S(1)}, u32[]{:S(2)}, u32[]{:S(2)}) collective-permute-start(f32[25,1,768]{2,0,1:T(8,128)S(1)} %copy.963), channel_id=1, source_target_pairs={{0,1},{1,2},{2,3},{3,4},{4,5},{5,6},{6,7},{7,8},{8,9},{9,10},{10,1... | collective-permute-start | bytes 230408 | tf_op jit(solution)/shard_map/ppermute | solution.py:26
  88.4 14.8 %copy-start = (f32[4,8,6,512]{3,1,2,0:T(8,128)}, f32[4,8,6,512]{3,1,2,0:T(8,128)S(1)}, u32[]{:S(2)}) copy-start(f32[4,8,6,512]{3,1,2,0:T(8,128)S(1)} %copy.1005) | copy-start | bytes 1179652
  88.4 4.2 %copy-start.56 = (pred[1536]{0:T(1024)(128)(4,1)S(1)}, pred[1536]{0:T(1024)(128)(4,1)}, u32[]{:S(2)}) copy-start(pred[1536]{0:T(1024)(128)(4,1)} %copy-done.54) | copy-start | bytes 4612
  94.0 7.6 %copy-start.26 = (bf16[1,125,256]{2,0,1:T(2,128)(2,1)S(1)}, bf16[1,125,256]{2,0,1:T(2,128)(2,1)}, u32[]{:S(2)}) copy-start(bf16[1,125,256]{2,0,1:T(2,128)(2,1)} %get-tuple-element.689) | copy-start | bytes 192004
  94.0 7.6 %copy-start.82 = (f32[125,1]{0,1:T(1,128)S(1)}, f32[125,1]{0,1:T(1,128)}, u32[]{:S(2)}) copy-start(f32[125,1]{0,1:T(1,128)} %constant.1185) | copy-start | bytes 1504
  94.0 8.3 %copy-start.51 = (bf16[2,64,256]{2,1,0:T(8,128)(2,1)S(1)}, bf16[2,64,256]{2,1,0:T(8,128)(2,1)}, u32[]{:S(2)}) copy-start(bf16[2,64,256]{2,1,0:T(8,128)(2,1)} %param.139) | copy-start | bytes 196612
  94.0 8.3 %copy-start.84 = (f32[64,1]{0,1:T(1,128)S(1)}, f32[64,1]{0,1:T(1,128)}, u32[]{:S(2)}) copy-start(f32[64,1]{0,1:T(1,128)} %constant.1184) | copy-start | bytes 772
  94.4 8.7 %collective-permute-start.5 = (f32[25,1,768]{2,0,1:T(8,128)S(1)}, f32[25,1,768]{2,0,1:T(8,128)S(1)}, u32[]{:S(2)}, u32[]{:S(2)}) collective-permute-start(f32[25,1,768]{2,0,1:T(8,128)S(1)} %copy.975), channel_id=1, source_target_pairs={{1,0},{2,1},{3,2},{4,3},{5,4},{6,5},{7,6},{8,7},{9,8},{10,9},{11,1... | collective-permute-start | bytes 230408 | tf_op jit(solution)/shard_map/ppermute | solution.py:28
  99.4 3.8 %collective-permute-start.4 = (f32[25,1,768]{2,0,1:T(8,128)S(1)}, f32[25,1,768]{2,0,1:T(8,128)S(1)}, u32[]{:S(2)}, u32[]{:S(2)}) collective-permute-start(f32[25,1,768]{2,0,1:T(8,128)S(1)} %copy.974), channel_id=1, source_target_pairs={{0,1},{1,2},{2,3},{3,4},{4,5},{5,6},{6,7},{7,8},{8,9},{9,10},{10,1... | collective-permute-start | bytes 230408 | tf_op jit(solution)/shard_map/ppermute | solution.py:26
  123.7 3.5 %copy-start.4 = (f32[3,5,5,5,256]{4,2,1,3,0:T(8,128)}, f32[3,5,5,5,256]{4,2,1,3,0:T(8,128)S(1)}, u32[]{:S(2)}) copy-start(f32[3,5,5,5,256]{4,2,1,3,0:T(8,128)S(1)} %maximum_multiply_fusion.1) | copy-start | bytes 1152004
  133.8 7.4 %copy-start.30 = (f32[1,64,256]{2,1,0:T(8,128)S(1)}, f32[1,64,256]{2,1,0:T(8,128)}, u32[]{:S(2)}) copy-start(f32[1,64,256]{2,1,0:T(8,128)} %stack.126) | copy-start | bytes 196612
  133.8 7.4 %copy-start.31 = (f32[1,64,256]{2,1,0:T(8,128)S(1)}, f32[1,64,256]{2,1,0:T(8,128)}, u32[]{:S(2)}) copy-start(f32[1,64,256]{2,1,0:T(8,128)} %stack.124) | copy-start | bytes 196612
  133.8 7.4 %copy-start.32 = (f32[1,64,256]{2,1,0:T(8,128)S(1)}, f32[1,64,256]{2,1,0:T(8,128)}, u32[]{:S(2)}) copy-start(f32[1,64,256]{2,1,0:T(8,128)} %stack.125) | copy-start | bytes 196612
  133.9 7.4 %copy-start.62 = (f32[256]{0:T(256)S(1)}, f32[256]{0:T(256)}, u32[]{:S(2)}) copy-start(f32[256]{0:T(256)} %copy-done.58) | copy-start | bytes 3076
  133.9 8.1 %copy-start.20 = (f32[1,125,256]{2,1,0:T(8,128)S(1)}, f32[1,125,256]{2,1,0:T(8,128)}, u32[]{:S(2)}) copy-start(f32[1,125,256]{2,1,0:T(8,128)} %stack.129) | copy-start | bytes 384004
  133.9 8.1 %copy-start.21 = (f32[1,125,256]{2,1,0:T(8,128)S(1)}, f32[1,125,256]{2,1,0:T(8,128)}, u32[]{:S(2)}) copy-start(f32[1,125,256]{2,1,0:T(8,128)} %stack.128) | copy-start | bytes 384004
  133.9 8.0 %copy-start.22 = (f32[1,125,256]{2,1,0:T(8,128)S(1)}, f32[1,125,256]{2,1,0:T(8,128)}, u32[]{:S(2)}) copy-start(f32[1,125,256]{2,1,0:T(8,128)} %stack.130) | copy-start | bytes 384004
  133.9 8.0 %copy-start.67 = (f32[256]{0:T(256)S(1)}, f32[256]{0:T(256)}, u32[]{:S(2)}) copy-start(f32[256]{0:T(256)} %copy-done.63) | copy-start | bytes 3076
  134.3 8.6 %collective-permute-start.7 = (f32[25,1,768]{2,0,1:T(8,128)S(1)}, f32[25,1,768]{2,0,1:T(8,128)S(1)}, u32[]{:S(2)}, u32[]{:S(2)}) collective-permute-start(f32[25,1,768]{2,0,1:T(8,128)S(1)} %copy.987), channel_id=1, source_target_pairs={{1,0},{2,1},{3,2},{4,3},{5,4},{6,5},{7,6},{8,7},{9,8},{10,9},{11,1... | collective-permute-start | bytes 230408 | tf_op jit(solution)/shard_map/ppermute | solution.py:28
  139.3 3.8 %collective-permute-start.6 = (f32[25,1,768]{2,0,1:T(8,128)S(1)}, f32[25,1,768]{2,0,1:T(8,128)S(1)}, u32[]{:S(2)}, u32[]{:S(2)}) collective-permute-start(f32[25,1,768]{2,0,1:T(8,128)S(1)} %copy.986), channel_id=1, source_target_pairs={{0,1},{1,2},{2,3},{3,4},{4,5},{5,6},{6,7},{7,8},{8,9},{9,10},{10,1... | collective-permute-start | bytes 230408 | tf_op jit(solution)/shard_map/ppermute | solution.py:26
  162.8 17.5 %copy-start.13 = (f32[3,64,256]{2,1,0:T(8,128)S(1)}, f32[3,64,256]{2,1,0:T(8,128)}, u32[]{:S(2)}) copy-start(f32[3,64,256]{2,1,0:T(8,128)} %maximum_multiply_fusion.5) | copy-start | bytes 589828
  166.8 15.3 %collective-permute-start.8 = (f32[512]{0:T(512)S(1)}, f32[512]{0:T(512)S(1)}, u32[]{:S(2)}, u32[]{:S(2)}) collective-permute-start(f32[512]{0:T(512)S(1)} %get-tuple-element.715), channel_id=1, source_target_pairs={{2,0},{3,1},{4,2},{5,3},{6,4},{7,5},{8,6},{9,7},{10,8},{11,9},{12,... | collective-permute-start | bytes 6152 | tf_op jit(solution)/shard_map/ppermute | solution.py:38
  170.8 11.3 %collective-permute-start.11 = (f32[512]{0:T(512)S(1)}, f32[512]{0:T(512)S(1)}, u32[]{:S(2)}, u32[]{:S(2)}) collective-permute-start(f32[512]{0:T(512)S(1)} %get-tuple-element.716), channel_id=1, source_target_pairs={{0,2},{1,3},{2,4},{3,5},{4,6},{5,7},{6,8},{7,9},{8,10},{9,11},{10,... | collective-permute-start | bytes 6152 | tf_op jit(solution)/shard_map/ppermute | solution.py:38
  172.8 9.2 %collective-permute-start.10 = (f32[512]{0:T(512)S(1)}, f32[512]{0:T(512)S(1)}, u32[]{:S(2)}, u32[]{:S(2)}) collective-permute-start(f32[512]{0:T(512)S(1)} %get-tuple-element.717), channel_id=1, source_target_pairs={{0,1},{1,2},{2,3},{3,4},{4,5},{5,6},{6,7},{7,8},{8,9},{9,10},{10,1... | collective-permute-start | bytes 6152 | tf_op jit(solution)/shard_map/ppermute | solution.py:38
  178.3 4.9 %collective-permute-start.9 = (f32[512]{0:T(512)S(1)}, f32[512]{0:T(512)S(1)}, u32[]{:S(2)}, u32[]{:S(2)}) collective-permute-start(f32[512]{0:T(512)S(1)} %get-tuple-element.718), channel_id=1, source_target_pairs={{1,0},{2,1},{3,2},{4,3},{5,4},{6,5},{7,6},{8,7},{9,8},{10,9},{11,1... | collective-permute-start | bytes 6152 | tf_op jit(solution)/shard_map/ppermute | solution.py:38
  (56 other events, 110.0 us)
where the time goes:
time: 186 us; the launch traced here: 184 us
  local copies, waits for them, and re-layouts  93.2 us (50%)
  starting transfers between devices  38.7 us (21%)
  matrix products  24.5 us (13%)
  other arithmetic  20.6 us (11%)
  between operations  3.82 us (2%)
  waiting for transfers between devices  2.97 us (2%)
    gather x8, local copies, waits for them, and re-layouts, neighbour_traces(): picked = jnp.take(trace_table, jnp.maximum(flat_link, 0), axis=1)  51 us
    dot_general x24, matrix products, derive_along(): return jnp.einsum(patterns[direction], matrix, field, precision=HIGHEST)  16.8 us
    ppermute x4, starting transfers between devices, padded(): lax.ppermute(head, axis, [((i + 1) % count, i) for i in range(ends)])  14.6 us
    ppermute x4, starting transfers between devices, shifted(): return lax.ppermute(block, axis, route)  13.3 us
    gather x4, local copies, waits for them, and re-layouts, pick_sent(): jnp.take(own_traces, send_faces.reshape(-1), axis=1)  12.5 us
    ppermute x4, starting transfers between devices, padded(): lax.ppermute(tail, axis, [(i, (i + 1) % count) for i in range(ends)])  10.7 us
    concatenate x4, local copies, waits for them, and re-layouts, neighbour_traces(): trace_table = jnp.concatenate([own_traces, remote], axis=1)  7.03 us
    unnamed x226, local copies, waits for them, and re-layouts  4.76 us
  transfers between devices with their start and end apart: 12, of which 4 were waited for; matrix products, arithmetic and copies ran while one was open for 8% of the time, Pallas kernels for 0%

commit v1 on v0

v1 whole, which is shorter than its diff:
```python
import functools
import math

import jax
import jax.numpy as jnp
import ml_dtypes
import numpy as np
from jax import lax
from jax.experimental import pallas as pl
from jax.experimental.pallas import tpu as pltpu
from jax.sharding import PartitionSpec as P

STEPS = 2
TIME_STEP = 0.02
SOURCE_WEIGHT = (45.0 / 32.0) ** 3
HIGHEST = lax.Precision.HIGHEST
TILE = 128
ROWS = 32
CENTRE = 62


def gll_points(degree):
    if degree == 3:
        interior = math.sqrt(0.2)
        return np.array([-1.0, -interior, interior, 1.0])
    interior = math.sqrt(3.0 / 7.0)
    return np.array([-1.0, -interior, 0.0, interior, 1.0])


def gll_weights(degree):
    if degree == 3:
        return np.array([1.0 / 6.0, 5.0 / 6.0, 5.0 / 6.0, 1.0 / 6.0])
    return np.array([0.1, 49.0 / 90.0, 32.0 / 45.0, 49.0 / 90.0, 0.1])


def lagrange_table(targets, sources):
    result = np.ones((targets.shape[0], sources.shape[0]))
    for col in range(sources.shape[0]):
        for skip in range(sources.shape[0]):
            if skip != col:
                result[:, col] *= (targets - sources[skip]) / (sources[col] - sources[skip])
    return result


def derivative_table(degree):
    points = gll_points(degree)
    number = points.shape[0]
    barycentric = np.ones(number)
    for col in range(number):
        for skip in range(number):
            if skip != col:
                barycentric[col] /= points[col] - points[skip]
    result = np.zeros((number, number))
    for row in range(number):
        for col in range(number):
            if row != col:
                result[row, col] = barycentric[col] / barycentric[row] / (points[row] - points[col])
        result[row, row] = -np.sum(result[row])
    return result


def halves(matrix):
    high = matrix.astype(ml_dtypes.bfloat16)
    low = (matrix - high.astype(np.float64)).astype(ml_dtypes.bfloat16)
    return high, low


def face_nodes(n, face):
    cube = np.arange(n**3).reshape(n, n, n)
    return np.take(cube, 0 if face % 2 == 0 else n - 1, axis=face // 2).reshape(-1)


def order_tables(degree):
    n = degree + 1
    nodes = 64 if degree == 3 else 128
    lift = 6.0 if degree == 3 else 10.0
    exact = degree == 4
    points, mortar = gll_points(degree), gll_points(4)
    up = np.eye(5) if exact else lagrange_table(mortar, points)
    down = np.eye(5) if exact else lagrange_table(points, mortar)
    up, down = np.kron(up, up), np.kron(down, down)
    trace = np.zeros((6, ROWS, nodes))
    place = np.zeros((6, nodes, ROWS))
    for face in range(6):
        at = face_nodes(n, face)
        trace[face, :25, at] = up.T
        place[face, at, :25] = down
    pressure_trace = trace.reshape(6 * ROWS, nodes)
    sign = np.array([-1.0, 1.0] * 3)
    velocity_trace = (sign[:, None, None] * trace).reshape(3, 2 * ROWS, nodes)
    diff = derivative_table(degree)
    move_v, move_p = [], []
    for a in range(3):
        parts = [np.eye(n)] * 3
        parts[a] = diff
        own = np.zeros((nodes, nodes))
        own[: n**3, : n**3] = np.kron(np.kron(parts[0], parts[1]), parts[2])
        for side in range(2):
            at = face_nodes(n, 2 * a + side)
            own[at, at] += 0.5 * lift * (1 - 2 * side)
        own_hi, own_lo = halves(own)
        for rows, first in ((move_v, -1.0), (move_p, -1.0)):
            second = 1.0 if rows is move_v else -1.0
            other = 0.5 * lift * np.concatenate([first * place[2 * a], second * place[2 * a + 1]], 1)
            hi, lo = halves(other)
            rows.append(np.concatenate([own_hi, own_hi, own_lo, hi, hi] + ([] if exact else [lo]), 1))

    def spread(matrix):
        hi, lo = halves(matrix)
        return np.concatenate([hi, hi] + ([] if exact else [lo]), -1)

    weights = gll_weights(degree)
    cube = (weights[:, None, None] * weights[None, :, None] * weights[None, None, :]).reshape(-1)
    cube = np.repeat(cube[:, None], 256, 1).astype(np.float32)
    return spread(pressure_trace), spread(velocity_trace), np.stack(move_v), np.stack(move_p), cube


def split(value):
    high = value.astype(jnp.bfloat16)
    return high, (value - high.astype(jnp.float32)).astype(jnp.bfloat16)


def times(matrix, pieces):
    return jnp.dot(matrix, jnp.concatenate(pieces, axis=0), preferred_element_type=jnp.float32)


def picked(index, sources, start):
    lane = index & (TILE - 1)
    tile = index >> 7
    parts = list(start)
    for k, ref in sources:
        here = tile == k
        for row in range(ROWS // 8):
            block = ref[8 * row : 8 * row + 8, :]
            found = jnp.take_along_axis(block, lane, axis=1, mode="promise_in_bounds")
            parts[row] = jnp.where(here, found, parts[row])
    return parts


def kernel(
    n,
    state_low, state_high, forward_low, forward_high, bulk, buoyancy, stretch, live, link, send,
    receiver, residual, cell,
    tp_low, tp_high, tv_low, tv_high, mv_low, mv_high, mp_low, mp_high, weight_low, weight_high,
    out_low, out_high, grad,
    p_low, v_low, p_high, v_high, table, outgoing, remote, nb_low, nb_high, source, terms, wanted,
    blocks, arrived, send_sem, recv_sem, gsend_sem, grecv_sem,
):
    me = lax.axis_index("domain")
    slots = state_low.shape[2]
    side_tiles = outgoing.shape[1]
    barrier = pltpu.get_barrier_semaphore()
    count = 0
    for distance in (-2, -1, 1, 2):
        there = me + distance
        exists = jnp.logical_and(there >= 0, there < n)
        count = count + exists.astype(jnp.int32)

        @pl.when(exists)
        def _():
            pl.semaphore_signal(
                barrier, inc=1, device_id={"domain": there}, device_id_type=pl.DeviceIdType.MESH
            )

    @pl.when(me == 0)
    def _():
        remote[:, 0] = jnp.zeros(remote[:, 0].shape, jnp.float32)

    @pl.when(me == n - 1)
    def _():
        remote[:, 1] = jnp.zeros(remote[:, 1].shape, jnp.float32)

    for block in (0, 1, 3, 4):
        origin = me - (block - 2)

        @pl.when(jnp.logical_or(origin < 0, origin >= n))
        def _():
            arrived[block] = jnp.zeros(arrived[block].shape, jnp.float32)

    slot = lax.broadcasted_iota(jnp.int32, (1, slots), 1)
    alive_low = (slot < live[0:1, 0:1]).astype(jnp.float32)
    alive_high = (slot < live[1:2, 0:1]).astype(jnp.float32)
    p_high[120:128, :] = jnp.zeros((8, slots), jnp.float32)
    p_low[...] = state_low[0] * alive_low
    p_high[0:125, :] = state_high[0] * alive_high
    for a in range(3):
        v_high[a, 120:128, :] = jnp.zeros((8, slots), jnp.float32)
        v_low[a] = state_low[1 + a] * alive_low
        v_high[a, 0:125, :] = state_high[1 + a] * alive_high
    stretch_low, stretch_high = stretch[:, :slots], stretch[:, slots:]
    rate_v_low = TIME_STEP * buoyancy[:, :slots] * stretch_low * alive_low
    rate_v_high = TIME_STEP * buoyancy[:, slots:] * stretch_high * alive_high
    rate_p_low = TIME_STEP * bulk[:, :slots] * stretch_low * alive_low
    rate_p_high = TIME_STEP * bulk[:, slots:] * stretch_high * alive_high
    volume_low = stretch_low * stretch_low * stretch_low
    volume_high = stretch_high * stretch_high * stretch_high
    rows = lax.broadcasted_iota(jnp.int32, (TILE, receiver.shape[1]), 0)
    at_slot = (rows == receiver[...]).astype(jnp.float32)
    shared = lax.dot_general(
        jnp.concatenate([residual[...]] * 4, axis=0), at_slot, (((1,), (1,)), ((), ())), precision=HIGHEST,
        preferred_element_type=jnp.float32,
    )
    shared = shared * (
        TIME_STEP * SOURCE_WEIGHT * bulk[:, slots : slots + TILE] * volume_high[:, :TILE]
    )
    for t in range(STEPS):
        source[t] = shared[t : t + 1]
    terms[...] = jnp.zeros(terms.shape, jnp.float32)
    for face in range(6):
        for quarter in range(4):
            wanted[face, quarter] = jnp.broadcast_to(
                link[face : face + 1, quarter * TILE : (quarter + 1) * TILE], (8, TILE)
            )

    pl.semaphore_wait(barrier, count)

    def copy_down(turn):
        return pltpu.make_async_remote_copy(
            src_ref=outgoing.at[0], dst_ref=remote.at[turn, 1],
            send_sem=send_sem.at[turn, 0], recv_sem=recv_sem.at[turn, 1],
            device_id={"domain": me - 1}, device_id_type=pl.DeviceIdType.MESH,
        )

    def copy_up(turn):
        return pltpu.make_async_remote_copy(
            src_ref=outgoing.at[1], dst_ref=remote.at[turn, 0],
            send_sem=send_sem.at[turn, 1], recv_sem=recv_sem.at[turn, 0],
            device_id={"domain": me + 1}, device_id_type=pl.DeviceIdType.MESH,
        )

    def exchange(turn, traces_low, traces_high):
        for face in range(6):
            for half in range(2):
                lanes = slice(half * TILE, (half + 1) * TILE)
                faces = slice(face * ROWS, (face + 1) * ROWS)
                table[4 * face + half] = traces_low[faces, lanes]
                table[4 * face + 2 + half] = traces_high[faces, lanes]
        lower = [(k, table.at[k]) for k in range(0, 24, 2)]
        blank = [jnp.zeros((8, TILE), jnp.float32)] * (ROWS // 8)
        for way in range(2):

            def pick_out(m, carry):
                at = pl.multiple_of(m * TILE, TILE)
                index = jnp.broadcast_to(send[way : way + 1, pl.ds(at, TILE)], (8, TILE))
                parts = picked(index, lower, blank)
                for row in range(ROWS // 8):
                    outgoing[way, m, 8 * row : 8 * row + 8, :] = parts[row]
                return carry

            lax.fori_loop(0, side_tiles, pick_out, 0)
            if way == 0:

                @pl.when(me > 0)
                def _():
                    copy_down(turn).start()
            else:

                @pl.when(me < n - 1)
                def _():
                    copy_up(turn).start()

        own = [(k, table.at[k]) for k in range(24)]

        def pick_own(face, carry):
            for quarter in range(4):
                into = nb_low if quarter < 2 else nb_high
                lanes = slice((quarter % 2) * TILE, (quarter % 2 + 1) * TILE)
                parts = picked(wanted[face, quarter], own, blank)
                for row in range(ROWS // 8):
                    into[face, 8 * row : 8 * row + 8, lanes] = parts[row]
            return carry

        lax.fori_loop(0, 6, pick_own, 0)

        @pl.when(me > 0)
        def _():
            copy_down(turn).wait_send()
            copy_up(turn).wait_recv()

        @pl.when(me < n - 1)
        def _():
            copy_up(turn).wait_send()
            copy_down(turn).wait_recv()

        far = [(24 + m, remote.at[turn, m // side_tiles, m % side_tiles]) for m in range(2 * side_tiles)]

        def pick_far(face, carry):
            for quarter in (0, 2):
                into = nb_low if quarter < 2 else nb_high
                start = [into[face, 8 * row : 8 * row + 8, :TILE] for row in range(ROWS // 8)]
                parts = picked(wanted[face, quarter], far, start)
                for row in range(ROWS // 8):
                    into[face, 8 * row : 8 * row + 8, :TILE] = parts[row]
            return carry

        lax.fori_loop(0, 6, pick_far, 0)

    def neighbours(a):
        low_hi, low_lo = split(nb_low[2 * a : 2 * a + 2].reshape(2 * ROWS, slots))
        high_hi, high_lo = split(nb_high[2 * a : 2 * a + 2].reshape(2 * ROWS, slots))
        return [low_hi, low_lo, low_hi], [high_hi, high_lo]

    def step(t, carry):
        low_hi, low_lo = split(p_low[...])
        high_hi, high_lo = split(p_high[...])
        exchange(
            2 * t,
            times(tp_low[...], [low_hi, low_lo, low_hi]),
            times(tp_high[...], [high_hi, high_lo]),
        )
        traces_low, traces_high = [], []
        for a in range(3):
            from_low, from_high = neighbours(a)
            pl_hi, pl_lo = split(p_low[...])
            ph_hi, ph_lo = split(p_high[...])
            new_low = v_low[a] - rate_v_low * times(mv_low[a], [pl_hi, pl_lo, pl_hi] + from_low)
            new_high = v_high[a] - rate_v_high * times(mv_high[a], [ph_hi, ph_lo, ph_hi] + from_high)
            v_low[a] = new_low
            v_high[a] = new_high
            low_hi, low_lo = split(new_low)
            high_hi, high_lo = split(new_high)
            traces_low.append(times(tv_low[a], [low_hi, low_lo, low_hi]))
            traces_high.append(times(tv_high[a], [high_hi, high_lo]))
        exchange(2 * t + 1, jnp.concatenate(traces_low, 0), jnp.concatenate(traces_high, 0))
        total_low, total_high = 0.0, 0.0
        for a in range(3):
            from_low, from_high = neighbours(a)
            low_hi, low_lo = split(v_low[a])
            high_hi, high_lo = split(v_high[a])
            total_low = total_low + times(mp_low[a], [low_hi, low_lo, low_hi] + from_low)
            total_high = total_high + times(mp_high[a], [high_hi, high_lo, high_hi] + from_high)
        p_low[...] = p_low[...] - rate_p_low * total_low
        p_high[...] = p_high[...] - rate_p_high * total_high
        p_high[CENTRE : CENTRE + 1, :TILE] = (
            p_high[CENTRE : CENTRE + 1, :TILE] + source[t]
        )
        weighted_low = weight_low[...] * forward_low[t].astype(jnp.float32) * p_low[...]
        weighted_high = weight_high[...] * forward_high[t].astype(jnp.float32) * p_high[0:125, :]
        terms[:, :slots] += jnp.sum(weighted_low, axis=0, keepdims=True) / volume_low
        terms[:, slots:] += jnp.sum(weighted_high, axis=0, keepdims=True) / volume_high
        return carry

    lax.fori_loop(0, STEPS, step, 0)

    cells = 2 * slots
    relative = cell[...] - (me - 2) * cells
    group = relative >> 7
    group = (group >> 2) * 8 + (group & 3)
    spread_terms = jnp.where(
        lax.broadcasted_iota(jnp.int32, (40, cells), 0) == group, terms[...], 0.0
    )
    lane = (lax.broadcasted_iota(jnp.int32, (TILE, cells), 0) == (relative & (TILE - 1))).astype(
        jnp.float32
    )
    window = lax.dot_general(
        spread_terms, lane, (((1,), (1,)), ((), ())), precision=HIGHEST,
        preferred_element_type=jnp.float32,
    )
    blocks[...] = window.reshape(5, 8, TILE)

    def gradient_copy(block):
        return pltpu.make_async_remote_copy(
            src_ref=blocks.at[block], dst_ref=arrived.at[block],
            send_sem=gsend_sem.at[block], recv_sem=grecv_sem.at[block],
            device_id={"domain": me + (block - 2)}, device_id_type=pl.DeviceIdType.MESH,
        )

    for block in (0, 4, 1, 3):
        there = me + (block - 2)

        @pl.when(jnp.logical_and(there >= 0, there < n))
        def _():
            gradient_copy(block).start()

    out_low[0] = p_low[...]
    out_high[0] = p_high[0:125, :]
    for a in range(3):
        out_low[1 + a] = v_low[a]
        out_high[1 + a] = v_high[a, 0:125, :]
    for block in (0, 4, 1, 3):
        there = me + (block - 2)
        origin = me - (block - 2)

        @pl.when(jnp.logical_and(there >= 0, there < n))
        def _():
            gradient_copy(block).wait_send()

        @pl.when(jnp.logical_and(origin >= 0, origin < n))
        def _():
            gradient_copy(block).wait_recv()

    total = blocks[2]
    for block in (0, 1, 3, 4):
        total = total + arrived[block]
    grad[...] = total[:4]


def shards(n, state_low, state_high, forward_low, forward_high, bulk_modulus, buoyancy, stretch,
           live_count, face_link, send_faces, receiver_slot, residual, model_cell):
    tp_low, tv_low, mv_low, mp_low, weight_low = order_tables(3)
    tp_high, tv_high, mv_high, mp_high, weight_high = order_tables(4)
    tables = [tp_low, tp_high, tv_low, tv_high, mv_low, mv_high, mp_low, mp_high, weight_low, weight_high]
    slots = state_low.shape[2]
    side_tiles = send_faces.shape[1] // TILE
    vmem = pl.BlockSpec(memory_space=pltpu.VMEM)
    out_low, out_high, grad = pl.pallas_call(
        functools.partial(kernel, n),
        out_shape=(
            jax.ShapeDtypeStruct(state_low.shape, jnp.float32),
            jax.ShapeDtypeStruct(state_high.shape, jnp.float32),
            jax.ShapeDtypeStruct((2 * slots // TILE, TILE), jnp.float32),
        ),
        in_specs=[vmem] * (13 + len(tables)),
        out_specs=(vmem, vmem, vmem),
        scratch_shapes=[
            pltpu.VMEM((64, slots), jnp.float32),
            pltpu.VMEM((3, 64, slots), jnp.float32),
            pltpu.VMEM((128, slots), jnp.float32),
            pltpu.VMEM((3, 128, slots), jnp.float32),
            pltpu.VMEM((24, ROWS, TILE), jnp.float32),
            pltpu.VMEM((2, side_tiles, ROWS, TILE), jnp.float32),
            pltpu.VMEM((2 * STEPS, 2, side_tiles, ROWS, TILE), jnp.float32),
            pltpu.VMEM((6, ROWS, slots), jnp.float32),
            pltpu.VMEM((6, ROWS, slots), jnp.float32),
            pltpu.VMEM((STEPS, 1, TILE), jnp.float32),
            pltpu.VMEM((1, 2 * slots), jnp.float32),
            pltpu.VMEM((6, 4, 8, TILE), jnp.int32),
            pltpu.VMEM((5, 8, TILE), jnp.float32),
            pltpu.VMEM((5, 8, TILE), jnp.float32),
            pltpu.SemaphoreType.DMA((2 * STEPS, 2)),
            pltpu.SemaphoreType.DMA((2 * STEPS, 2)),
            pltpu.SemaphoreType.DMA((5,)),
            pltpu.SemaphoreType.DMA((5,)),
        ],
        compiler_params=pltpu.CompilerParams(
            collective_id=0, has_side_effects=True, vmem_limit_bytes=32 * 1024 * 1024
        ),
    )(
        state_low, state_high, forward_low, forward_high, bulk_modulus.reshape(1, -1),
        buoyancy.reshape(1, -1), stretch.reshape(1, -1), live_count, face_link, send_faces,
        receiver_slot.reshape(1, -1), residual, model_cell.reshape(1, -1),
        *[jnp.asarray(table) for table in tables],
    )
    return out_low, out_high, grad.reshape(-1)


def solution(mesh):
    placed = (
        P("groups", None, "domain"),
        P("groups", None, "domain"),
        P("groups", None, "domain"),
        P("groups", None, "domain"),
        P("domain"),
        P("domain"),
        P("domain"),
        P(None, "domain"),
        P(None, "domain"),
        P(None, "domain"),
        P("domain"),
        P("groups", "domain"),
        P("domain"),
    )
    return jax.shard_map(
        functools.partial(shards, mesh.shape["domain"]),
        mesh=mesh,
        in_specs=placed,
        out_specs=(
            P("groups", None, "domain"),
            P("groups", None, "domain"),
            P(("groups", "domain")),
        ),
        check_vma=False,
    )
```

time: 186 us -> 50.9 us (0.27)
  local copies, waits for them, and re-layouts: 93.2 us -> 16.3 us
  starting transfers between devices: 38.7 us -> 0 us
  Pallas kernels: 0 us -> 33.3 us
  matrix products: 24.5 us -> 0 us
  other arithmetic: 20.6 us -> 0 us
  between operations: 3.82 us -> 0.76 us
  waiting for transfers between devices: 2.97 us -> 0 us
    gather x12 -> x0, local copies, waits for them, and re-layouts: 63.5 us -> none  [the longest x8 51 us: neighbour_traces(): picked = jnp.take(trace_table, jnp.maximum(flat_link, 0), axis=1)]
    ppermute x12 -> x0, starting transfers between devices: 38.7 us -> none  [the longest x4 14.6 us: padded(): lax.ppermute(head, axis, [((i + 1) % count, i) for i in range(ends)])]
    pallas_call x0 -> x1, Pallas kernels: none -> 33.3 us  [shards(): pl.pallas_call(functools.partial(kernel, n), out_shape=(jax.ShapeDtypeStr...]
    dot_general x44 -> x0, matrix products: 24.5 us -> none  [the longest x24 16.8 us: derive_along(): return jnp.einsum(patterns[direction], matrix, field, precision=HIGHEST)]
    unnamed x226 -> x48, local copies, waits for them, and re-layouts: 4.76 us -> 16.3 us
    concatenate x8 -> x0, local copies, waits for them, and re-layouts: 7.77 us -> none  [the longest x4 7.03 us: neighbour_traces(): trace_table = jnp.concatenate([own_traces, remote], axis=1)]
    scatter-add x3 -> x0, other arithmetic: 6.24 us -> none  [the longest x1 3.39 us: shards(): jnp.zeros((5 * CELL_DEV,), jnp.float32).at[model_cell - window_base]]
    slice x28 -> x0, local copies, waits for them, and re-layouts: 5.95 us -> none  [the longest x1 1.37 us: start_state(): pressure_high = state_high[0].reshape(5, 5, 5, slot_total) * alive_high]
  transfers between devices with their start and end apart: 12 -> 0, of which waited for: 4 -> 0; matrix products, arithmetic and copies ran while one was open for 8% -> 0% of each run, Pallas kernels for 0% -> 0%
where the time goes in v1:
time: 50.9 us; the launch traced here: 50.4 us
  Pallas kernels  33.3 us (65%)
  local copies, waits for them, and re-layouts  16.3 us (32%)
  between operations  0.76 us (1%)
    pallas_call x1, Pallas kernels, shards(): pl.pallas_call(functools.partial(kernel, n), out_shape=(jax.ShapeDtypeStr...  33.3 us
    unnamed x48, local copies, waits for them, and re-layouts  16.3 us

profile of v1, /device:TPU:19, one launch (start us, length us, event | category | flops | bytes accessed | tf_op | source)
XLA Modules:
  0.0 50.4 jit_solution(2395500597101214647)
XLA Ops:
  0.6 0.0 copy-start.20
  0.6 0.6 %copy-done.20 = s32[2,1]{0,1:T(1,128)S(1)} copy-done((s32[2,1]{0,1:T(1,128)S(1)}, s32[2,1]{0,1:T(1,128)}, u32[]{:S(2)}) %copy-start.20) | copy-done | bytes 32
  1.3 0.1 copy.28.live
  1.4 0.0 copy-start.2
  1.4 1.0 %copy.27.forward_high = bf16[2,125,256]{2,1,0:T(8,128)(2,1)S(1)} copy(bf16[2,125,256]{2,0,1:T(2,128)(2,1)} %param.26) | data formatting | bytes 256000 | tf_op args[3]
  2.3 0.0 copy-start
  2.4 0.0 copy-start.1
  2.4 0.0 copy-start.3
  2.4 0.0 copy-start.6
  2.4 0.0 copy-start.18
  2.4 1.2 %copy.26.state_high = f32[4,125,256]{2,1,0:T(8,128)S(1)} copy(f32[4,125,256]{2,0,1:T(4,128)} %param.24) | data formatting | bytes 1024000 | tf_op args[1]
  3.6 0.0 copy-done.2
  3.6 0.0 copy-done
  3.6 0.0 copy-done.1
  3.7 0.0 copy-done.3
  3.7 0.0 copy-done.6
  3.7 0.0 copy-done.18
  3.7 0.0 copy-start.4
  3.7 0.9 %copy-done.4 = bf16[3,64,384]{2,1,0:T(8,128)(2,1)S(1)} copy-done((bf16[3,64,384]{2,1,0:T(8,128)(2,1)S(1)}, bf16[3,64,384]{2,1,0:T(8,128)(2,1)}, u32[]{:S(2)}) %copy-start.4) | copy-done | bytes 147480
  4.6 0.0 copy-start.5
  4.6 0.9 %copy-done.5 = f32[125,256]{1,0:T(8,128)S(1)} copy-done((f32[125,256]{1,0:T(8,128)S(1)}, f32[125,256]{1,0:T(8,128)}, u32[]{:S(2)}) %copy-start.5) | copy-done | bytes 128024
  5.5 0.0 copy-start.7
  5.5 0.9 %copy-done.7 = bf16[3,64,192]{2,1,0:T(8,128)(2,1)S(1)} copy-done((bf16[3,64,192]{2,1,0:T(8,128)(2,1)S(1)}, bf16[3,64,192]{2,1,0:T(8,128)(2,1)}, u32[]{:S(2)}) %copy-start.7) | copy-done | bytes 73752
  6.4 0.0 copy-start.8
  6.4 0.9 %copy-done.8 = bf16[192,256]{1,0:T(8,128)(2,1)S(1)} copy-done((bf16[192,256]{1,0:T(8,128)(2,1)S(1)}, bf16[192,256]{1,0:T(8,128)(2,1)}, u32[]{:S(2)}) %copy-start.8) | copy-done | bytes 98328
  7.3 0.9 %copy-done.9 = bf16[192,192]{1,0:T(8,128)(2,1)S(1)} copy-done((bf16[192,192]{1,0:T(8,128)(2,1)S(1)}, bf16[192,192]{1,0:T(8,128)(2,1)}, u32[]{:S(2)}) %copy-start.9) | copy-done | bytes 73752
  8.2 0.0 copy-start.10
  8.2 0.8 %copy-done.10 = bf16[2,64,256]{2,1,0:T(8,128)(2,1)S(1)} copy-done((bf16[2,64,256]{2,1,0:T(8,128)(2,1)S(1)}, bf16[2,64,256]{2,1,0:T(8,128)(2,1)}, u32[]{:S(2)}) %copy-start.10) | copy-done | bytes 65560
  9.0 0.0 copy-start.11
  9.0 0.8 %copy-done.11 = f32[64,256]{1,0:T(8,128)S(1)} copy-done((f32[64,256]{1,0:T(8,128)S(1)}, f32[64,256]{1,0:T(8,128)}, u32[]{:S(2)}) %copy-start.11) | copy-done | bytes 65560
  9.9 0.0 copy-start.12
  9.9 0.7 %copy-done.12 = s32[6,512]{1,0:T(8,128)S(1)} copy-done((s32[6,512]{1,0:T(8,128)S(1)}, s32[6,512]{1,0:T(8,128)}, u32[]{:S(2)}) %copy-start.12) | copy-done | bytes 12312
  10.6 0.0 copy-start.13
  10.6 0.7 %copy-done.13 = s32[2,768]{1,0:T(2,128)S(1)} copy-done((s32[2,768]{1,0:T(2,128)S(1)}, s32[2,768]{1,0:T(2,128)}, u32[]{:S(2)}) %copy-start.13) | copy-done | bytes 6168
  11.3 0.0 copy-start.14
  11.3 0.7 %copy-done.14 = f32[512]{0:T(512)S(1)} copy-done((f32[512]{0:T(512)S(1)}, f32[512]{0:T(512)}, u32[]{:S(2)}) %copy-start.14) | copy-done | bytes 2072
  12.0 0.0 copy-start.15
  12.0 0.7 %copy-done.15 = f32[512]{0:T(512)S(1)} copy-done((f32[512]{0:T(512)S(1)}, f32[512]{0:T(512)}, u32[]{:S(2)}) %copy-start.15) | copy-done | bytes 2072
  12.6 0.0 copy-start.16
  12.6 0.7 %copy-done.16 = f32[512]{0:T(512)S(1)} copy-done((f32[512]{0:T(512)S(1)}, f32[512]{0:T(512)}, u32[]{:S(2)}) %copy-start.16) | copy-done | bytes 2072
  13.3 0.0 copy-start.17
  13.3 0.7 %copy-done.17 = s32[512]{0:T(512)S(1)} copy-done((s32[512]{0:T(512)S(1)}, s32[512]{0:T(512)}, u32[]{:S(2)}) %copy-start.17) | copy-done | bytes 2072
  14.0 0.0 copy-start.19
  14.0 0.7 %copy-done.19 = s32[128]{0:T(128)S(1)} copy-done((s32[128]{0:T(128)S(1)}, s32[128]{0:T(128)}, u32[]{:S(2)}) %copy-start.19) | copy-done | bytes 536
  14.7 33.3 %shard_map.238 = (f32[4,64,256]{2,1,0:T(8,128)S(1)}, f32[4,125,256]{2,1,0:T(8,128)S(1)}, f32[4,128]{1,0:T(4,128)S(1)}) custom-call(f32[4,64,256]{2,1,0:T(8,128)S(1)} %copy-done.2, f32[4,125,256]{2,1,0:T(8,128)S(1)} %copy.26.state_high, bf16[2,64,256]{2,1,0:T(8,128)(2,1)S(1)} %copy-done.10, bf16[2,125,256]{2,1,0:T(8,128)(2,1)S(1)} %copy.27.forward_high, ...), custom_call_target="tpu_custom_call" | custom-call | tf_op jit(solution)/shard_map/pallas_call | solution.py:406
  48.0 1.1 %copy.29 = f32[4,125,256]{2,0,1:T(4,128)} copy(f32[4,125,256]{2,1,0:T(8,128)S(1)} %get-tuple-element.10) | data formatting | bytes 1024000
  49.1 0.7 %copy.32 = f32[4,64,256]{2,1,0:T(8,128)} copy(f32[4,64,256]{2,1,0:T(8,128)S(1)} %get-tuple-element.15) | data formatting | bytes 524288
  49.8 0.6 %copy.33 = f32[512]{0:T(512)} copy(f32[512]{0:T(512)S(1)} %bitcast.6) | data formatting | bytes 4096
  (1 shorter events, 0.0 us)
Async XLA Ops:
  0.6 0.7 %copy-start.20 = (s32[2,1]{0,1:T(1,128)S(1)}, s32[2,1]{0,1:T(1,128)}, u32[]{:S(2)}) copy-start(s32[2,1]{0,1:T(1,128)} %param.30) | copy-start | bytes 28
  1.4 2.3 %copy-start.2 = (f32[4,64,256]{2,1,0:T(8,128)S(1)}, f32[4,64,256]{2,1,0:T(8,128)}, u32[]{:S(2)}) copy-start(f32[4,64,256]{2,1,0:T(8,128)} %state_low.1) | copy-start | bytes 786436
  2.3 1.3 %copy-start = (bf16[3,128,512]{2,1,0:T(8,128)(2,1)S(1)}, bf16[3,128,512]{2,1,0:T(8,128)(2,1)}, u32[]{:S(2)}) copy-start(bf16[3,128,512]{2,1,0:T(8,128)(2,1)} %constant.27.clone.mp_high) | copy-start | bytes 1179652
  2.4 1.3 %copy-start.1 = (bf16[3,128,512]{2,1,0:T(8,128)(2,1)S(1)}, bf16[3,128,512]{2,1,0:T(8,128)(2,1)}, u32[]{:S(2)}) copy-start(bf16[3,128,512]{2,1,0:T(8,128)(2,1)} %constant.25.clone.mv_high) | copy-start | bytes 1179652
  2.4 1.3 %copy-start.3 = (bf16[3,64,384]{2,1,0:T(8,128)(2,1)S(1)}, bf16[3,64,384]{2,1,0:T(8,128)(2,1)}, u32[]{:S(2)}) copy-start(bf16[3,64,384]{2,1,0:T(8,128)(2,1)} %constant.26.clone.mp_low) | copy-start | bytes 442372
  2.4 1.3 %copy-start.6 = (bf16[3,64,256]{2,1,0:T(8,128)(2,1)S(1)}, bf16[3,64,256]{2,1,0:T(8,128)(2,1)}, u32[]{:S(2)}) copy-start(bf16[3,64,256]{2,1,0:T(8,128)(2,1)} %constant.23.clone.tv_high) | copy-start | bytes 294916
  2.4 1.3 %copy-start.18 = (f32[2,128]{1,0:T(2,128)S(1)}, f32[2,128]{1,0:T(2,128)}, u32[]{:S(2)}) copy-start(f32[2,128]{1,0:T(2,128)} %residual.1) | copy-start | bytes 3076
  3.7 0.9 %copy-start.4 = (bf16[3,64,384]{2,1,0:T(8,128)(2,1)S(1)}, bf16[3,64,384]{2,1,0:T(8,128)(2,1)}, u32[]{:S(2)}) copy-start(bf16[3,64,384]{2,1,0:T(8,128)(2,1)} %constant.24.clone.mv_low) | copy-start | bytes 442372
  4.6 0.9 %copy-start.5 = (f32[125,256]{1,0:T(8,128)S(1)}, f32[125,256]{1,0:T(8,128)}, u32[]{:S(2)}) copy-start(f32[125,256]{1,0:T(8,128)} %constant.29.clone.weight_high) | copy-start | bytes 384004
  5.5 0.9 %copy-start.7 = (bf16[3,64,192]{2,1,0:T(8,128)(2,1)S(1)}, bf16[3,64,192]{2,1,0:T(8,128)(2,1)}, u32[]{:S(2)}) copy-start(bf16[3,64,192]{2,1,0:T(8,128)(2,1)} %constant.22.clone.tv_low) | copy-start | bytes 221188
  6.4 0.9 %copy-start.8 = (bf16[192,256]{1,0:T(8,128)(2,1)S(1)}, bf16[192,256]{1,0:T(8,128)(2,1)}, u32[]{:S(2)}) copy-start(bf16[192,256]{1,0:T(8,128)(2,1)} %constant.21.clone.tp_high) | copy-start | bytes 294916
  7.3 0.9 %copy-start.9 = (bf16[192,192]{1,0:T(8,128)(2,1)S(1)}, bf16[192,192]{1,0:T(8,128)(2,1)}, u32[]{:S(2)}) copy-start(bf16[192,192]{1,0:T(8,128)(2,1)} %constant.20.clone.tp_low) | copy-start | bytes 221188
  8.2 0.8 %copy-start.10 = (bf16[2,64,256]{2,1,0:T(8,128)(2,1)S(1)}, bf16[2,64,256]{2,1,0:T(8,128)(2,1)}, u32[]{:S(2)}) copy-start(bf16[2,64,256]{2,1,0:T(8,128)(2,1)} %forward_low.1) | copy-start | bytes 196612
  9.0 0.8 %copy-start.11 = (f32[64,256]{1,0:T(8,128)S(1)}, f32[64,256]{1,0:T(8,128)}, u32[]{:S(2)}) copy-start(f32[64,256]{1,0:T(8,128)} %constant.28.clone.weight_low) | copy-start | bytes 196612
  9.9 0.7 %copy-start.12 = (s32[6,512]{1,0:T(8,128)S(1)}, s32[6,512]{1,0:T(8,128)}, u32[]{:S(2)}) copy-start(s32[6,512]{1,0:T(8,128)} %link.1) | copy-start | bytes 36868
  10.6 0.7 %copy-start.13 = (s32[2,768]{1,0:T(2,128)S(1)}, s32[2,768]{1,0:T(2,128)}, u32[]{:S(2)}) copy-start(s32[2,768]{1,0:T(2,128)} %send.1) | copy-start | bytes 18436
  11.3 0.7 %copy-start.14 = (f32[512]{0:T(512)S(1)}, f32[512]{0:T(512)}, u32[]{:S(2)}) copy-start(f32[512]{0:T(512)} %param.27) | copy-start | bytes 6148
  12.0 0.7 %copy-start.15 = (f32[512]{0:T(512)S(1)}, f32[512]{0:T(512)}, u32[]{:S(2)}) copy-start(f32[512]{0:T(512)} %param.28) | copy-start | bytes 6148
  12.6 0.7 %copy-start.16 = (f32[512]{0:T(512)S(1)}, f32[512]{0:T(512)}, u32[]{:S(2)}) copy-start(f32[512]{0:T(512)} %param.29) | copy-start | bytes 6148
  13.3 0.7 %copy-start.17 = (s32[512]{0:T(512)S(1)}, s32[512]{0:T(512)}, u32[]{:S(2)}) copy-start(s32[512]{0:T(512)} %param.35) | copy-start | bytes 6148
  14.0 0.7 %copy-start.19 = (s32[128]{0:T(128)S(1)}, s32[128]{0:T(128)}, u32[]{:S(2)}) copy-start(s32[128]{0:T(128)} %param.33) | copy-start | bytes 1540

commit v2 on v1

--- a/solution.py
+++ b/solution.py
@@ -15,7 +15,10 @@
 SOURCE_WEIGHT = (45.0 / 32.0) ** 3
 HIGHEST = lax.Precision.HIGHEST
 TILE = 128
-ROWS = 32
+ROWS = 24
+FACE_ROWS = 6 * ROWS + 8
+LOAD_ORDER = tuple(range(21))
+VMEM_GRANT = 63 * 1024 * 1024
 CENTRE = 62
 
 
@@ -79,15 +82,22 @@
     up = np.eye(5) if exact else lagrange_table(mortar, points)
     down = np.eye(5) if exact else lagrange_table(points, mortar)
     up, down = np.kron(up, up), np.kron(down, down)
-    trace = np.zeros((6, ROWS, nodes))
-    place = np.zeros((6, nodes, ROWS))
+    sign = np.array([-1.0, 1.0] * 3)
+    pressure_trace = np.zeros((FACE_ROWS, nodes))
+    velocity_trace = np.zeros((3, FACE_ROWS, nodes))
+    place = np.zeros((6, nodes, 25))
     for face in range(6):
         at = face_nodes(n, face)
-        trace[face, :25, at] = up.T
-        place[face, at, :25] = down
-    pressure_trace = trace.reshape(6 * ROWS, nodes)
-    sign = np.array([-1.0, 1.0] * 3)
-    velocity_trace = (sign[:, None, None] * trace).reshape(3, 2 * ROWS, nodes)
+        rows = np.append(face * ROWS + np.arange(ROWS), 6 * ROWS + face)
+        pressure_trace[np.ix_(rows, at)] = up
+        velocity_trace[face // 2][np.ix_(rows, at)] = sign[face] * up
+        place[face, at] = down
+    velocity_trace = np.concatenate(
+        [
+            np.concatenate([velocity_trace[a, 2 * a * ROWS : 2 * (a + 1) * ROWS], velocity_trace[a, 6 * ROWS :]])
+            for a in range(3)
+        ]
+    ).reshape(3, 2 * ROWS + 8, nodes)
     diff = derivative_table(degree)
     move_v, move_p = [], []
     for a in range(3):
@@ -101,7 +111,11 @@
         own_hi, own_lo = halves(own)
         for rows, first in ((move_v, -1.0), (move_p, -1.0)):
             second = 1.0 if rows is move_v else -1.0
-            other = 0.5 * lift * np.concatenate([first * place[2 * a], second * place[2 * a + 1]], 1)
+            other = np.zeros((nodes, 64))
+            for side, factor in enumerate((first, second)):
+                column = side * ROWS
+                other[:, column : column + ROWS] = 0.5 * lift * factor * place[2 * a + side][:, :ROWS]
+                other[:, 2 * ROWS + 2 * a + side] = 0.5 * lift * factor * place[2 * a + side][:, ROWS]
             hi, lo = halves(other)
             rows.append(np.concatenate([own_hi, own_hi, own_lo, hi, hi] + ([] if exact else [lo]), 1))
 
@@ -124,31 +138,53 @@
     return jnp.dot(matrix, jnp.concatenate(pieces, axis=0), preferred_element_type=jnp.float32)
 
 
-def picked(index, sources, start):
+def picked(index, sources, lasts, start, last):
     lane = index & (TILE - 1)
     tile = index >> 7
     parts = list(start)
-    for k, ref in sources:
+    for k, load in sources:
         here = tile == k
         for row in range(ROWS // 8):
-            block = ref[8 * row : 8 * row + 8, :]
-            found = jnp.take_along_axis(block, lane, axis=1, mode="promise_in_bounds")
+            found = jnp.take_along_axis(load(row), lane, axis=1, mode="promise_in_bounds")
             parts[row] = jnp.where(here, found, parts[row])
-    return parts
+    sublane = lax.broadcasted_iota(jnp.int32, (8, TILE), 0)
+    for first, stride, load in lasts:
+        found = jnp.take_along_axis(load(), lane, axis=1, mode="promise_in_bounds")
+        last = jnp.where(tile == first + stride * sublane, found, last)
+    return parts, last
 
 
 def kernel(
-    n,
-    state_low, state_high, forward_low, forward_high, bulk, buoyancy, stretch, live, link, send,
+    n, live, *refs
+):
+    count = 21
+    hbm, outs, vmem = refs[:count], refs[count : count + 3], refs[count + 3 : 2 * count + 3]
+    body(n, live, hbm, *vmem, *outs, *refs[2 * count + 3 :])
+
+
+def body(
+    n, live, hbm,
+    state_low, state_high, forward_low, forward_high, bulk, buoyancy, stretch, link, send,
     receiver, residual, cell,
-    tp_low, tp_high, tv_low, tv_high, mv_low, mv_high, mp_low, mp_high, weight_low, weight_high,
+    tables_low, tables_high, tv_low, tv_high, mv_low, mv_high, mp_low, mp_high, weights,
     out_low, out_high, grad,
-    p_low, v_low, p_high, v_high, table, outgoing, remote, nb_low, nb_high, source, terms, wanted,
-    blocks, arrived, send_sem, recv_sem, gsend_sem, grecv_sem,
+    p_low, v_low, p_high, v_high, table, outgoing, remote, near, near_last, source, terms, wanted,
+    blocks, arrived, send_sem, recv_sem, gsend_sem, grecv_sem, load_sem,
 ):
     me = lax.axis_index("domain")
+    held = (
+        state_low, state_high, forward_low, forward_high, bulk, buoyancy, stretch, link, send,
+        receiver, residual, cell,
+        tables_low, tables_high, tv_low, tv_high, mv_low, mv_high, mp_low, mp_high, weights,
+    )
+    loads = [
+        pltpu.make_async_copy(source_ref, target, load_sem.at[i])
+        for i, (source_ref, target) in enumerate(zip(hbm, held))
+    ]
+    for i in LOAD_ORDER:
+        loads[i].start()
     slots = state_low.shape[2]
-    side_tiles = outgoing.shape[1]
+    side_tiles = send.shape[1] // TILE
     barrier = pltpu.get_barrier_semaphore()
     count = 0
     for distance in (-2, -1, 1, 2):
@@ -177,9 +213,11 @@
         def _():
             arrived[block] = jnp.zeros(arrived[block].shape, jnp.float32)
 
+    for load in loads:
+        load.wait()
     slot = lax.broadcasted_iota(jnp.int32, (1, slots), 1)
-    alive_low = (slot < live[0:1, 0:1]).astype(jnp.float32)
-    alive_high = (slot < live[1:2, 0:1]).astype(jnp.float32)
+    alive_low = (slot < live[0, 0]).astype(jnp.float32)
+    alive_high = (slot < live[0, 1]).astype(jnp.float32)
     p_high[120:128, :] = jnp.zeros((8, slots), jnp.float32)
     p_low[...] = state_low[0] * alive_low
     p_high[0:125, :] = state_high[0] * alive_high
@@ -229,25 +267,32 @@
         )
 
     def exchange(turn, traces_low, traces_high):
-        for face in range(6):
-            for half in range(2):
-                lanes = slice(half * TILE, (half + 1) * TILE)
-                faces = slice(face * ROWS, (face + 1) * ROWS)
-                table[4 * face + half] = traces_low[faces, lanes]
-                table[4 * face + 2 + half] = traces_high[faces, lanes]
-        lower = [(k, table.at[k]) for k in range(0, 24, 2)]
-        blank = [jnp.zeros((8, TILE), jnp.float32)] * (ROWS // 8)
+        for quarter, traces in enumerate((traces_low, traces_low, traces_high, traces_high)):
+            table[quarter] = traces[:, (quarter % 2) * TILE : (quarter % 2 + 1) * TILE]
+
+        def load_own(k):
+            return lambda row: table[k % 4, (k // 4) * ROWS + 8 * row : (k // 4) * ROWS + 8 * row + 8, :]
+
+        def load_own_last(quarter):
+            return lambda: table[quarter, 6 * ROWS :, :]
+
+        lower = [(k, load_own(k)) for k in range(0, 24, 2)]
+        lower_last = [(quarter, 4, load_own_last(quarter)) for quarter in (0, 2)]
+        zero = jnp.zeros((8, TILE), jnp.float32)
+        blank = [zero] * (ROWS // 8)
+        sublane = lax.broadcasted_iota(jnp.int32, (8, TILE), 0)
         for way in range(2):
 
-            def pick_out(m, carry):
+            def pick_out(m, lasts):
                 at = pl.multiple_of(m * TILE, TILE)
                 index = jnp.broadcast_to(send[way : way + 1, pl.ds(at, TILE)], (8, TILE))
-                parts = picked(index, lower, blank)
+                parts, last = picked(index, lower, lower_last, blank, zero)
                 for row in range(ROWS // 8):
-                    outgoing[way, m, 8 * row : 8 * row + 8, :] = parts[row]
-                return carry
-
-            lax.fori_loop(0, side_tiles, pick_out, 0)
+                    into = pl.multiple_of(m * ROWS + 8 * row, 8)
+                    outgoing[way, pl.ds(into, 8), :] = parts[row]
+                return jnp.where(sublane == m, jnp.sum(last, axis=0, keepdims=True), lasts)
+
+            outgoing[way, side_tiles * ROWS :, :] = lax.fori_loop(0, side_tiles, pick_out, zero)
             if way == 0:
 
                 @pl.when(me > 0)
@@ -259,18 +304,23 @@
                 def _():
                     copy_up(turn).start()
 
-        own = [(k, table.at[k]) for k in range(24)]
-
-        def pick_own(face, carry):
+        own = [(k, load_own(k)) for k in range(24)]
+        own_last = [(quarter, 4, load_own_last(quarter)) for quarter in range(4)]
+
+        def pick_own(face, lasts):
+            result = []
             for quarter in range(4):
-                into = nb_low if quarter < 2 else nb_high
-                lanes = slice((quarter % 2) * TILE, (quarter % 2 + 1) * TILE)
-                parts = picked(wanted[face, quarter], own, blank)
+                parts, last = picked(wanted[face, quarter], own, own_last, blank, zero)
                 for row in range(ROWS // 8):
-                    into[face, 8 * row : 8 * row + 8, lanes] = parts[row]
-            return carry
-
-        lax.fori_loop(0, 6, pick_own, 0)
+                    near[quarter, face, 8 * row : 8 * row + 8, :] = parts[row]
+                result.append(
+                    jnp.where(sublane == face, jnp.sum(last, axis=0, keepdims=True), lasts[quarter])
+                )
+            return tuple(result)
+
+        lasts = lax.fori_loop(0, 6, pick_own, (zero,) * 4)
+        for quarter in range(4):
+            near_last[quarter] = lasts[quarter]
 
         @pl.when(me > 0)
         def _():
@@ -282,31 +332,64 @@
             copy_up(turn).wait_send()
             copy_down(turn).wait_recv()
 
-        far = [(24 + m, remote.at[turn, m // side_tiles, m % side_tiles]) for m in range(2 * side_tiles)]
-
-        def pick_far(face, carry):
-            for quarter in (0, 2):
-                into = nb_low if quarter < 2 else nb_high
-                start = [into[face, 8 * row : 8 * row + 8, :TILE] for row in range(ROWS // 8)]
-                parts = picked(wanted[face, quarter], far, start)
+        def load_far(m):
+            way, first = m // side_tiles, (m % side_tiles) * ROWS
+            return lambda row: remote[turn, way, first + 8 * row : first + 8 * row + 8, :]
+
+        def load_far_last(way):
+            return lambda: remote[turn, way, side_tiles * ROWS :, :]
+
+        far = [(24 + m, load_far(m)) for m in range(2 * side_tiles)]
+        far_last = [(24 + way * side_tiles, 1, load_far_last(way)) for way in range(2)]
+
+        def pick_far(face, lasts):
+            result = []
+            for place, quarter in enumerate((0, 2)):
+                start = [near[quarter, face, 8 * row : 8 * row + 8, :] for row in range(ROWS // 8)]
+                parts, last = picked(wanted[face, quarter], far, far_last, start, zero)
                 for row in range(ROWS // 8):
-                    into[face, 8 * row : 8 * row + 8, :TILE] = parts[row]
-            return carry
-
-        lax.fori_loop(0, 6, pick_far, 0)
+                    near[quarter, face, 8 * row : 8 * row + 8, :] = parts[row]
+                result.append(
+                    jnp.where(sublane == face, jnp.sum(last, axis=0, keepdims=True), lasts[place])
+                )
+            return tuple(result)
+
+        lasts = lax.fori_loop(0, 6, pick_far, (zero,) * 2)
+        near_last[0] += lasts[0]
+        near_last[2] += lasts[1]
 
     def neighbours(a):
-        low_hi, low_lo = split(nb_low[2 * a : 2 * a + 2].reshape(2 * ROWS, slots))
-        high_hi, high_lo = split(nb_high[2 * a : 2 * a + 2].reshape(2 * ROWS, slots))
+        pieces = []
+        for order in range(2):
+            sides = []
+            for half in range(2):
+                quarter = 2 * order + half
+                sides.append(
+                    jnp.concatenate(
+                        [
+                            near[quarter, 2 * a],
+                            near[quarter, 2 * a + 1],
+                            near_last[quarter],
+                            jnp.zeros((8, TILE), jnp.float32),
+                        ],
+                        axis=0,
+                    )
+                )
+            pieces.append(split(jnp.concatenate(sides, axis=1)))
+        (low_hi, low_lo), (high_hi, high_lo) = pieces
         return [low_hi, low_lo, low_hi], [high_hi, high_lo]
+
+    def joined(traces):
+        faces = [trace[: 2 * ROWS] for trace in traces]
+        return jnp.concatenate(faces + [sum(trace[2 * ROWS :] for trace in traces)], axis=0)
 
     def step(t, carry):
         low_hi, low_lo = split(p_low[...])
         high_hi, high_lo = split(p_high[...])
         exchange(
             2 * t,
-            times(tp_low[...], [low_hi, low_lo, low_hi]),
-            times(tp_high[...], [high_hi, high_lo]),
+            times(tables_low[...], [low_hi, low_lo, low_hi]),
+            times(tables_high[...], [high_hi, high_lo]),
         )
         traces_low, traces_high = [], []
         for a in range(3):
@@ -321,7 +404,7 @@
             high_hi, high_lo = split(new_high)
             traces_low.append(times(tv_low[a], [low_hi, low_lo, low_hi]))
             traces_high.append(times(tv_high[a], [high_hi, high_lo]))
-        exchange(2 * t + 1, jnp.concatenate(traces_low, 0), jnp.concatenate(traces_high, 0))
+        exchange(2 * t + 1, joined(traces_low), joined(traces_high))
         total_low, total_high = 0.0, 0.0
         for a in range(3):
             from_low, from_high = neighbours(a)
@@ -334,8 +417,8 @@
         p_high[CENTRE : CENTRE + 1, :TILE] = (
             p_high[CENTRE : CENTRE + 1, :TILE] + source[t]
         )
-        weighted_low = weight_low[...] * forward_low[t].astype(jnp.float32) * p_low[...]
-        weighted_high = weight_high[...] * forward_high[t].astype(jnp.float32) * p_high[0:125, :]
+        weighted_low = weights[0:64] * forward_low[t].astype(jnp.float32) * p_low[...]
+        weighted_high = weights[64:189] * forward_high[t].astype(jnp.float32) * p_high[0:125, :]
         terms[:, :slots] += jnp.sum(weighted_low, axis=0, keepdims=True) / volume_low
         terms[:, slots:] += jnp.sum(weighted_high, axis=0, keepdims=True) / volume_high
         return carry
@@ -399,10 +482,16 @@
            live_count, face_link, send_faces, receiver_slot, residual, model_cell):
     tp_low, tv_low, mv_low, mp_low, weight_low = order_tables(3)
     tp_high, tv_high, mv_high, mp_high, weight_high = order_tables(4)
-    tables = [tp_low, tp_high, tv_low, tv_high, mv_low, mv_high, mp_low, mp_high, weight_low, weight_high]
+    tables = [tp_low, tp_high, tv_low, tv_high, mv_low, mv_high, mp_low, mp_high, np.concatenate([weight_low, weight_high])]
     slots = state_low.shape[2]
     side_tiles = send_faces.shape[1] // TILE
     vmem = pl.BlockSpec(memory_space=pltpu.VMEM)
+    operands = [
+        state_low, state_high, forward_low, forward_high, bulk_modulus.reshape(1, -1),
+        buoyancy.reshape(1, -1), stretch.reshape(1, -1), face_link, send_faces,
+        receiver_slot.reshape(1, -1), residual, model_cell.reshape(1, -1),
+        *[jnp.asarray(table) for table in tables],
+    ]
     out_low, out_high, grad = pl.pallas_call(
         functools.partial(kernel, n),
         out_shape=(
@@ -410,18 +499,19 @@
             jax.ShapeDtypeStruct(state_high.shape, jnp.float32),
             jax.ShapeDtypeStruct((2 * slots // TILE, TILE), jnp.float32),
         ),
-        in_specs=[vmem] * (13 + len(tables)),
+        in_specs=[pl.BlockSpec(memory_space=pltpu.SMEM)] + [pl.BlockSpec(memory_space=pl.ANY)] * len(operands),
         out_specs=(vmem, vmem, vmem),
         scratch_shapes=[
+            *[pltpu.VMEM(operand.shape, operand.dtype) for operand in operands],
             pltpu.VMEM((64, slots), jnp.float32),
             pltpu.VMEM((3, 64, slots), jnp.float32),
             pltpu.VMEM((128, slots), jnp.float32),
             pltpu.VMEM((3, 128, slots), jnp.float32),
-            pltpu.VMEM((24, ROWS, TILE), jnp.float32),
-            pltpu.VMEM((2, side_tiles, ROWS, TILE), jnp.float32),
-            pltpu.VMEM((2 * STEPS, 2, side_tiles, ROWS, TILE), jnp.float32),
-            pltpu.VMEM((6, ROWS, slots), jnp.float32),
-            pltpu.VMEM((6, ROWS, slots), jnp.float32),
+            pltpu.VMEM((4, FACE_ROWS, TILE), jnp.float32),
+            pltpu.VMEM((2, side_tiles * ROWS + 8, TILE), jnp.float32),
+            pltpu.VMEM((2 * STEPS, 2, side_tiles * ROWS + 8, TILE), jnp.float32),
+            pltpu.VMEM((4, 6, ROWS, TILE), jnp.float32),
+            pltpu.VMEM((4, 8, TILE), jnp.float32),
             pltpu.VMEM((STEPS, 1, TILE), jnp.float32),
             pltpu.VMEM((1, 2 * slots), jnp.float32),
             pltpu.VMEM((6, 4, 8, TILE), jnp.int32),
@@ -431,16 +521,12 @@
             pltpu.SemaphoreType.DMA((2 * STEPS, 2)),
             pltpu.SemaphoreType.DMA((5,)),
             pltpu.SemaphoreType.DMA((5,)),
+            pltpu.SemaphoreType.DMA((len(operands),)),
         ],
         compiler_params=pltpu.CompilerParams(
-            collective_id=0, has_side_effects=True, vmem_limit_bytes=32 * 1024 * 1024
+            collective_id=0, has_side_effects=True, vmem_limit_bytes=VMEM_GRANT
         ),
-    )(
-        state_low, state_high, forward_low, forward_high, bulk_modulus.reshape(1, -1),
-        buoyancy.reshape(1, -1), stretch.reshape(1, -1), live_count, face_link, send_faces,
-        receiver_slot.reshape(1, -1), residual, model_cell.reshape(1, -1),
-        *[jnp.asarray(table) for table in tables],
-    )
+    )(live_count.reshape(1, 2), *operands)
     return out_low, out_high, grad.reshape(-1)
 
 

time: 50.9 us -> 40.5 us (0.80)
  local copies, waits for them, and re-layouts: 16.3 us -> 6.99 us
  Pallas kernels: 33.3 us -> 32.6 us
    unnamed x48 -> x9, local copies, waits for them, and re-layouts: 16.3 us -> 6.99 us
    pallas_call x1, Pallas kernels: 33.3 us -> 32.6 us  [shards(): pl.pallas_call(functools.partial(kernel, n), out_shape=(jax.ShapeDtypeStr...]
where the time goes in v2:
time: 40.5 us; the launch traced here: 40.2 us
  Pallas kernels  32.6 us (80%)
  local copies, waits for them, and re-layouts  6.99 us (17%)
  between operations  0.65 us (2%)
    pallas_call x1, Pallas kernels, shards(): pl.pallas_call(functools.partial(kernel, n), out_shape=(jax.ShapeDtypeStr...  32.6 us
    unnamed x9, local copies, waits for them, and re-layouts  6.99 us

profile of v2, /device:TPU:19, one launch (start us, length us, event | category | flops | bytes accessed | tf_op | source)
XLA Modules:
  0.0 40.2 jit_solution(4911907697671591408)
XLA Ops:
  0.6 1.6 %copy.26.refs_3_ = bf16[2,125,256]{2,1,0:T(8,128)(2,1)} copy(bf16[2,125,256]{2,0,1:T(2,128)(2,1)} %param.25) | data formatting | bytes 256000 | tf_op args[3]
  2.2 1.9 %copy.25.refs_1_ = f32[4,125,256]{2,1,0:T(8,128)} copy(f32[4,125,256]{2,0,1:T(4,128)} %param.23) | data formatting | bytes 1024000 | tf_op args[1]
  4.1 32.6 %shard_map.229 = (f32[4,64,256]{2,1,0:T(8,128)}, f32[4,125,256]{2,1,0:T(8,128)}, f32[4,128]{1,0:T(4,128)}) custom-call(s32[1,2]{1,0:T(1,128)} %bitcast.12, f32[4,64,256]{2,1,0:T(8,128)} %refs_0_.1, f32[4,125,256]{2,1,0:T(8,128)} %copy.25.refs_1_, bf16[2,64,256]{2,1,0:T(8,128)(2,1)} %refs_2_.1, bf16[2,125,256]{2,1,0:T(8,128)(2,1)} %copy.26.refs_3_, ...), custom_call_target="tpu_custom_call" | custom-call | tf_op jit(solution)/shard_map/pallas_call | solution.py:495
  36.7 0.0 copy-start
  36.7 2.2 %copy.27 = f32[4,125,256]{2,0,1:T(4,128)} copy(f32[4,125,256]{2,1,0:T(8,128)} %get-tuple-element.10) | data formatting | bytes 1024000
  38.9 0.0 copy-done
  38.9 0.0 copy-start.1
  38.9 0.7 %copy.30 = f32[4,64,256]{2,1,0:T(8,128)} copy(f32[4,64,256]{2,1,0:T(8,128)S(1)} %copy-done) | data formatting | bytes 524288
  39.6 0.0 copy-done.1
  39.6 0.6 %copy.31 = f32[512]{0:T(512)} copy(f32[512]{0:T(512)S(1)} %bitcast.11) | data formatting | bytes 4096
Async XLA Ops:
  36.7 2.2 %copy-start = (f32[4,64,256]{2,1,0:T(8,128)S(1)}, f32[4,64,256]{2,1,0:T(8,128)}, u32[]{:S(2)}) copy-start(f32[4,64,256]{2,1,0:T(8,128)} %get-tuple-element.15) | copy-start | bytes 786436
  38.9 0.7 %copy-start.1 = (f32[4,128]{1,0:T(4,128)S(1)}, f32[4,128]{1,0:T(4,128)}, u32[]{:S(2)}) copy-start(f32[4,128]{1,0:T(4,128)} %get-tuple-element.8) | copy-start | bytes 6148

commit v3 on v2

--- a/solution.py
+++ b/solution.py
@@ -168,7 +168,7 @@
     receiver, residual, cell,
     tables_low, tables_high, tv_low, tv_high, mv_low, mv_high, mp_low, mp_high, weights,
     out_low, out_high, grad,
-    p_low, v_low, p_high, v_high, table, outgoing, remote, near, near_last, source, terms, wanted,
+    p_low, v_low, p_high, v_high, table, outgoing, remote, near, near_last, source, terms, wanted, rate, at_lane,
     blocks, arrived, send_sem, recv_sem, gsend_sem, grecv_sem, load_sem,
 ):
     me = lax.axis_index("domain")
@@ -219,12 +219,19 @@
     alive_low = (slot < live[0, 0]).astype(jnp.float32)
     alive_high = (slot < live[0, 1]).astype(jnp.float32)
     p_high[120:128, :] = jnp.zeros((8, slots), jnp.float32)
-    p_low[...] = state_low[0] * alive_low
-    p_high[0:125, :] = state_high[0] * alive_high
     for a in range(3):
         v_high[a, 120:128, :] = jnp.zeros((8, slots), jnp.float32)
+    rate[...] = forward_high[...].astype(jnp.float32)
+    p_low[...] = state_low[0] * alive_low
+    for half in range(2):
+        lanes = slice(half * TILE, (half + 1) * TILE)
+        p_high[0:125, lanes] = state_high[pl.ds(4 * half, 125, stride=8), :] * alive_high[:, lanes]
+        for a in range(3):
+            v_high[a, 0:125, lanes] = (
+                state_high[pl.ds(4 * half + 1 + a, 125, stride=8), :] * alive_high[:, lanes]
+            )
+    for a in range(3):
         v_low[a] = state_low[1 + a] * alive_low
-        v_high[a, 0:125, :] = state_high[1 + a] * alive_high
     stretch_low, stretch_high = stretch[:, :slots], stretch[:, slots:]
     rate_v_low = TIME_STEP * buoyancy[:, :slots] * stretch_low * alive_low
     rate_v_high = TIME_STEP * buoyancy[:, slots:] * stretch_high * alive_high
@@ -244,6 +251,13 @@
     for t in range(STEPS):
         source[t] = shared[t : t + 1]
     terms[...] = jnp.zeros(terms.shape, jnp.float32)
+    cells = 2 * slots
+    relative = cell[...] - (me - 2) * cells
+    group = relative >> 7
+    group = (group >> 2) * 8 + (group & 3)
+    at_lane[...] = jnp.where(
+        lax.broadcasted_iota(jnp.int32, (TILE, cells), 0) == (relative & (TILE - 1)), 1.0, 0.0
+    ).astype(jnp.bfloat16)
     for face in range(6):
         for quarter in range(4):
             wanted[face, quarter] = jnp.broadcast_to(
@@ -418,27 +432,29 @@
             p_high[CENTRE : CENTRE + 1, :TILE] + source[t]
         )
         weighted_low = weights[0:64] * forward_low[t].astype(jnp.float32) * p_low[...]
-        weighted_high = weights[64:189] * forward_high[t].astype(jnp.float32) * p_high[0:125, :]
+        forward_now = jnp.concatenate(
+            [rate[pl.ds(2 * half + t, 125, stride=4), :] for half in range(2)], axis=1
+        )
+        weighted_high = weights[64:189] * forward_now * p_high[0:125, :]
         terms[:, :slots] += jnp.sum(weighted_low, axis=0, keepdims=True) / volume_low
         terms[:, slots:] += jnp.sum(weighted_high, axis=0, keepdims=True) / volume_high
         return carry
 
     lax.fori_loop(0, STEPS, step, 0)
 
-    cells = 2 * slots
-    relative = cell[...] - (me - 2) * cells
-    group = relative >> 7
-    group = (group >> 2) * 8 + (group & 3)
-    spread_terms = jnp.where(
+    placed = jnp.where(
         lax.broadcasted_iota(jnp.int32, (40, cells), 0) == group, terms[...], 0.0
     )
-    lane = (lax.broadcasted_iota(jnp.int32, (TILE, cells), 0) == (relative & (TILE - 1))).astype(
-        jnp.float32
-    )
+    pieces = []
+    for _ in range(3):
+        pieces.append(placed.astype(jnp.bfloat16).astype(jnp.float32))
+        placed = placed - pieces[-1]
+    pieces.append(jnp.zeros((8, cells), jnp.float32))
     window = lax.dot_general(
-        spread_terms, lane, (((1,), (1,)), ((), ())), precision=HIGHEST,
-        preferred_element_type=jnp.float32,
-    )
+        jnp.concatenate(pieces, axis=0).astype(jnp.bfloat16), at_lane[...],
+        (((1,), (1,)), ((), ())), preferred_element_type=jnp.float32,
+    )
+    window = window[0:40] + window[40:80] + window[80:120]
     blocks[...] = window.reshape(5, 8, TILE)
 
     def gradient_copy(block):
@@ -456,10 +472,13 @@
             gradient_copy(block).start()
 
     out_low[0] = p_low[...]
-    out_high[0] = p_high[0:125, :]
     for a in range(3):
         out_low[1 + a] = v_low[a]
-        out_high[1 + a] = v_high[a, 0:125, :]
+    for half in range(2):
+        lanes = slice(half * TILE, (half + 1) * TILE)
+        out_high[pl.ds(4 * half, 125, stride=8), :] = p_high[0:125, lanes]
+        for a in range(3):
+            out_high[pl.ds(4 * half + 1 + a, 125, stride=8), :] = v_high[a, 0:125, lanes]
     for block in (0, 4, 1, 3):
         there = me + (block - 2)
         origin = me - (block - 2)
@@ -476,6 +495,11 @@
     for block in (0, 1, 3, 4):
         total = total + arrived[block]
     grad[...] = total[:4]
+
+
+def node_rows(values):
+    lead, nodes, slots = values.shape
+    return values.reshape(lead, nodes, slots // TILE, TILE).transpose(1, 2, 0, 3).reshape(-1, TILE)
 
 
 def shards(n, state_low, state_high, forward_low, forward_high, bulk_modulus, buoyancy, stretch,
@@ -487,7 +511,7 @@
     side_tiles = send_faces.shape[1] // TILE
     vmem = pl.BlockSpec(memory_space=pltpu.VMEM)
     operands = [
-        state_low, state_high, forward_low, forward_high, bulk_modulus.reshape(1, -1),
+        state_low, node_rows(state_high), forward_low, node_rows(forward_high), bulk_modulus.reshape(1, -1),
         buoyancy.reshape(1, -1), stretch.reshape(1, -1), face_link, send_faces,
         receiver_slot.reshape(1, -1), residual, model_cell.reshape(1, -1),
         *[jnp.asarray(table) for table in tables],
@@ -496,7 +520,7 @@
         functools.partial(kernel, n),
         out_shape=(
             jax.ShapeDtypeStruct(state_low.shape, jnp.float32),
-            jax.ShapeDtypeStruct(state_high.shape, jnp.float32),
+            jax.ShapeDtypeStruct((1000, TILE), jnp.float32),
             jax.ShapeDtypeStruct((2 * slots // TILE, TILE), jnp.float32),
         ),
         in_specs=[pl.BlockSpec(memory_space=pltpu.SMEM)] + [pl.BlockSpec(memory_space=pl.ANY)] * len(operands),
@@ -515,6 +539,8 @@
             pltpu.VMEM((STEPS, 1, TILE), jnp.float32),
             pltpu.VMEM((1, 2 * slots), jnp.float32),
             pltpu.VMEM((6, 4, 8, TILE), jnp.int32),
+            pltpu.VMEM((500, TILE), jnp.float32),
+            pltpu.VMEM((TILE, 2 * slots), jnp.bfloat16),
             pltpu.VMEM((5, 8, TILE), jnp.float32),
             pltpu.VMEM((5, 8, TILE), jnp.float32),
             pltpu.SemaphoreType.DMA((2 * STEPS, 2)),
@@ -527,6 +553,7 @@
             collective_id=0, has_side_effects=True, vmem_limit_bytes=VMEM_GRANT
         ),
     )(live_count.reshape(1, 2), *operands)
+    out_high = out_high.reshape(125, 2, 4, TILE).transpose(2, 0, 1, 3).reshape(state_high.shape)
     return out_low, out_high, grad.reshape(-1)
 
 

time: 40.5 us -> 38.1 us (0.941)
  local copies, waits for them, and re-layouts: 6.99 us -> 4.85 us
    unnamed x9 -> x7, local copies, waits for them, and re-layouts: 6.99 us -> 3.1 us
    reshape x0 -> x1, local copies, waits for them, and re-layouts: none -> 1.74 us  [node_rows(): values.reshape(lead, nodes, slots // TILE, TILE).transpose(1, 2, 0, 3)]
where the time goes in v3:
time: 38.1 us; the launch traced here: 37.9 us
  Pallas kernels  32.4 us (85%)
  local copies, waits for them, and re-layouts  4.85 us (13%)
  between operations  0.65 us (2%)
    pallas_call x1, Pallas kernels, shards(): pl.pallas_call(functools.partial(kernel, n), out_shape=(jax.ShapeDtypeStr...  32.4 us
    unnamed x7, local copies, waits for them, and re-layouts  3.1 us
    reshape x1, local copies, waits for them, and re-layouts, node_rows(): values.reshape(lead, nodes, slots // TILE, TILE).transpose(1, 2, 0, 3)  1.74 us

profile of v3, /device:TPU:19, one launch (start us, length us, event | category | flops | bytes accessed | tf_op | source)
XLA Modules:
  0.0 37.9 jit_solution(4470265378589013990)
XLA Ops:
  0.6 1.7 %reshape.49.refs_3_ = bf16[500,128]{1,0:T(8,128)(2,1)} reshape(bf16[125,2,2,128]{3,2,1,0:T(2,128)(2,1)} %bitcast.22) | data formatting | bytes 256000 | tf_op jit(solution)/shard_map/reshape | solution.py:502
  2.4 32.4 %shard_map.229 = (f32[4,64,256]{2,1,0:T(8,128)}, f32[1000,128]{1,0:T(8,128)}, f32[4,128]{1,0:T(4,128)}) custom-call(s32[1,2]{1,0:T(1,128)} %bitcast.28, f32[4,64,256]{2,1,0:T(8,128)} %refs_0_.1, f32[1000,128]{1,0:T(8,128)} %bitcast.21, bf16[2,64,256]{2,1,0:T(8,128)(2,1)} %refs_2_.1, bf16[500,128]{1,0:T(8,128)(2,1)} %reshape.49.refs_3_, f32[1,512]{1,0:T(1,128)} %bitcast.24, ...), custom_call_target="tpu_custom_call" | custom-call | tf_op jit(solution)/shard_map/pallas_call | solution.py:519
  34.8 0.0 copy-start
  34.8 1.7 %copy.31 = f32[4,64,256]{2,1,0:T(8,128)} copy(f32[4,64,256]{2,1,0:T(8,128)} %get-tuple-element.12) | data formatting | bytes 524288
  36.5 0.0 copy-done
  36.5 0.0 copy-start.1
  36.5 0.8 %copy.32 = f32[4,125,256]{2,0,1:T(4,128)} copy(f32[4,125,256]{2,0,1:T(4,128)S(1)} %bitcast.20) | data formatting | bytes 1024000
  37.3 0.0 copy-done.1
  37.3 0.6 %copy.33 = f32[512]{0:T(512)} copy(f32[512]{0:T(512)S(1)} %bitcast.23) | data formatting | bytes 4096
Async XLA Ops:
  34.8 1.7 %copy-start = (f32[1000,128]{1,0:T(8,128)S(1)}, f32[1000,128]{1,0:T(8,128)}, u32[]{:S(2)}) copy-start(f32[1000,128]{1,0:T(8,128)} %get-tuple-element.7) | copy-start | bytes 1536004
  36.5 0.8 %copy-start.1 = (f32[4,128]{1,0:T(4,128)S(1)}, f32[4,128]{1,0:T(4,128)}, u32[]{:S(2)}) copy-start(f32[4,128]{1,0:T(4,128)} %get-tuple-element.8) | copy-start | bytes 6148

commit v4 on v3

--- a/solution.py
+++ b/solution.py
@@ -159,17 +159,17 @@
 ):
     count = 21
     hbm, outs, vmem = refs[:count], refs[count : count + 3], refs[count + 3 : 2 * count + 3]
-    body(n, live, hbm, *vmem, *outs, *refs[2 * count + 3 :])
+    body(n, live, hbm, outs[:2], *vmem, outs[2], *refs[2 * count + 3 :])
 
 
 def body(
-    n, live, hbm,
+    n, live, hbm, final,
     state_low, state_high, forward_low, forward_high, bulk, buoyancy, stretch, link, send,
     receiver, residual, cell,
     tables_low, tables_high, tv_low, tv_high, mv_low, mv_high, mp_low, mp_high, weights,
-    out_low, out_high, grad,
+    grad, out_low, out_high,
     p_low, v_low, p_high, v_high, table, outgoing, remote, near, near_last, source, terms, wanted, rate, at_lane,
-    blocks, arrived, send_sem, recv_sem, gsend_sem, grecv_sem, load_sem,
+    blocks, arrived, send_sem, recv_sem, gsend_sem, grecv_sem, load_sem, store_sem,
 ):
     me = lax.axis_index("domain")
     held = (
@@ -221,7 +221,7 @@
     p_high[120:128, :] = jnp.zeros((8, slots), jnp.float32)
     for a in range(3):
         v_high[a, 120:128, :] = jnp.zeros((8, slots), jnp.float32)
-    rate[...] = forward_high[...].astype(jnp.float32)
+    rate[...] = forward_high[...].astype(jnp.float32).reshape(rate.shape)
     p_low[...] = state_low[0] * alive_low
     for half in range(2):
         lanes = slice(half * TILE, (half + 1) * TILE)
@@ -406,10 +406,10 @@
             times(tables_high[...], [high_hi, high_lo]),
         )
         traces_low, traces_high = [], []
+        pl_hi, pl_lo = split(p_low[...])
+        ph_hi, ph_lo = split(p_high[...])
         for a in range(3):
             from_low, from_high = neighbours(a)
-            pl_hi, pl_lo = split(p_low[...])
-            ph_hi, ph_lo = split(p_high[...])
             new_low = v_low[a] - rate_v_low * times(mv_low[a], [pl_hi, pl_lo, pl_hi] + from_low)
             new_high = v_high[a] - rate_v_high * times(mv_high[a], [ph_hi, ph_lo, ph_hi] + from_high)
             v_low[a] = new_low
@@ -474,11 +474,17 @@
     out_low[0] = p_low[...]
     for a in range(3):
         out_low[1 + a] = v_low[a]
+    stores = [
+        pltpu.make_async_copy(out_low, final[0], store_sem.at[0]),
+        pltpu.make_async_copy(out_high, final[1], store_sem.at[1]),
+    ]
+    stores[0].start()
     for half in range(2):
         lanes = slice(half * TILE, (half + 1) * TILE)
         out_high[pl.ds(4 * half, 125, stride=8), :] = p_high[0:125, lanes]
         for a in range(3):
             out_high[pl.ds(4 * half + 1 + a, 125, stride=8), :] = v_high[a, 0:125, lanes]
+    stores[1].start()
     for block in (0, 4, 1, 3):
         there = me + (block - 2)
         origin = me - (block - 2)
@@ -495,6 +501,8 @@
     for block in (0, 1, 3, 4):
         total = total + arrived[block]
     grad[...] = total[:4]
+    for store in stores:
+        store.wait()
 
 
 def node_rows(values):
@@ -511,7 +519,7 @@
     side_tiles = send_faces.shape[1] // TILE
     vmem = pl.BlockSpec(memory_space=pltpu.VMEM)
     operands = [
-        state_low, node_rows(state_high), forward_low, node_rows(forward_high), bulk_modulus.reshape(1, -1),
+        state_low, node_rows(state_high), forward_low, node_rows(forward_high).reshape(-1, STEPS, TILE), bulk_modulus.reshape(1, -1),
         buoyancy.reshape(1, -1), stretch.reshape(1, -1), face_link, send_faces,
         receiver_slot.reshape(1, -1), residual, model_cell.reshape(1, -1),
         *[jnp.asarray(table) for table in tables],
@@ -524,9 +532,11 @@
             jax.ShapeDtypeStruct((2 * slots // TILE, TILE), jnp.float32),
         ),
         in_specs=[pl.BlockSpec(memory_space=pltpu.SMEM)] + [pl.BlockSpec(memory_space=pl.ANY)] * len(operands),
-        out_specs=(vmem, vmem, vmem),
+        out_specs=(pl.BlockSpec(memory_space=pl.ANY), pl.BlockSpec(memory_space=pl.ANY), vmem),
         scratch_shapes=[
             *[pltpu.VMEM(operand.shape, operand.dtype) for operand in operands],
+            pltpu.VMEM(state_low.shape, jnp.float32),
+            pltpu.VMEM((1000, TILE), jnp.float32),
             pltpu.VMEM((64, slots), jnp.float32),
             pltpu.VMEM((3, 64, slots), jnp.float32),
             pltpu.VMEM((128, slots), jnp.float32),
@@ -548,6 +558,7 @@
             pltpu.SemaphoreType.DMA((5,)),
             pltpu.SemaphoreType.DMA((5,)),
             pltpu.SemaphoreType.DMA((len(operands),)),
+            pltpu.SemaphoreType.DMA((2,)),
         ],
         compiler_params=pltpu.CompilerParams(
             collective_id=0, has_side_effects=True, vmem_limit_bytes=VMEM_GRANT

time: 38.1 us -> 36.1 us (0.948)
  local copies, waits for them, and re-layouts: 4.85 us -> 3.1 us
    reshape x1 -> x0, local copies, waits for them, and re-layouts: 1.74 us -> none  [node_rows(): values.reshape(lead, nodes, slots // TILE, TILE).transpose(1, 2, 0, 3)]
where the time goes in v4:
time: 36.1 us; the launch traced here: 36 us
  Pallas kernels  32.2 us (89%)
  local copies, waits for them, and re-layouts  3.1 us (9%)
  between operations  0.65 us (2%)
    pallas_call x1, Pallas kernels, shards(): pl.pallas_call(functools.partial(kernel, n), out_shape=(jax.ShapeDtypeStr...  32.2 us
    unnamed x7, local copies, waits for them, and re-layouts  3.1 us

profile of v4, /device:TPU:19, one launch (start us, length us, event | category | flops | bytes accessed | tf_op | source)
XLA Modules:
  0.0 36.0 jit_solution(11964224994089617008)
XLA Ops:
  0.6 32.2 %shard_map.229 = (f32[4,64,256]{2,1,0:T(8,128)}, f32[1000,128]{1,0:T(8,128)}, f32[4,128]{1,0:T(4,128)}) custom-call(s32[1,2]{1,0:T(1,128)} %bitcast.30, f32[4,64,256]{2,1,0:T(8,128)} %refs_0_.1, f32[1000,128]{1,0:T(8,128)} %bitcast.22, bf16[2,64,256]{2,1,0:T(8,128)(2,1)} %refs_2_.1, bf16[250,2,128]{2,1,0:T(2,128)(2,1)} %bitcast.24, f32[1,512]{1,0:T(1,128)} %bitcast.25, ...), custom_call_target="tpu_custom_call" | custom-call | tf_op jit(solution)/shard_map/pallas_call | solution.py:527
  32.8 0.0 copy-start
  32.9 1.7 %copy.31 = f32[4,64,256]{2,1,0:T(8,128)} copy(f32[4,64,256]{2,1,0:T(8,128)} %get-tuple-element.12) | data formatting | bytes 524288
  34.6 0.0 copy-done
  34.6 0.0 copy-start.1
  34.6 0.8 %copy.32 = f32[4,125,256]{2,0,1:T(4,128)} copy(f32[4,125,256]{2,0,1:T(4,128)S(1)} %bitcast.23) | data formatting | bytes 1024000
  35.4 0.0 copy-done.1
  35.4 0.6 %copy.33 = f32[512]{0:T(512)} copy(f32[512]{0:T(512)S(1)} %bitcast.29) | data formatting | bytes 4096
Async XLA Ops:
  32.8 1.7 %copy-start = (f32[1000,128]{1,0:T(8,128)S(1)}, f32[1000,128]{1,0:T(8,128)}, u32[]{:S(2)}) copy-start(f32[1000,128]{1,0:T(8,128)} %get-tuple-element.7) | copy-start | bytes 1536004
  34.6 0.8 %copy-start.1 = (f32[4,128]{1,0:T(4,128)S(1)}, f32[4,128]{1,0:T(4,128)}, u32[]{:S(2)}) copy-start(f32[4,128]{1,0:T(4,128)} %get-tuple-element.8) | copy-start | bytes 6148
